TPU v7x, 512 devices: a whole 4x8x8 slice. The times are simulated.
512 devices in a mesh: row: 16 (over y, x_hi), col: 32 (over z, x_lo, core).
Axes of the slice: x: 4 (x_hi: 2, x_lo: 2; x = x_hi * 2 + x_lo), y: 8, z: 8, core: 2. Of those that a mesh axis runs over, the one named last changes fastest.
Arguments:
- pair: bfloat16 [768, 768, 128], P('row', 'col'), may hold values from -6 to 6
- token_mask: int32 [768], replicated, may hold values 0 or 1
- ln_gain: float32 [128], replicated, may hold values from 0.25 to 1.75
- ln_bias: float32 [128], replicated, may hold values from -3 to 3
- w_left: bfloat16 [128, 128], replicated, may hold values from -0.5 to 0.5
- w_right: bfloat16 [128, 128], replicated, may hold values from -0.5 to 0.5
- w_gate: bfloat16 [128, 128], replicated, may hold values from -0.5 to 0.5
- w_out: bfloat16 [64, 128], replicated, may hold values from -1.5 to 1.5
Outputs:
- update: bfloat16 [768, 768, 128], P('row', 'col')
All inputs are finite; a program needn't handle non-finite values.
Results may differ from a plain program's by a relative error of at most 0.0053.
Values may be sent and summed in bfloat16 or wider, within the bound.
A program may use at most 64 MiB of HBM per device.

v0:
```python
import math

import jax
import jax.numpy as jnp
from jax import lax
from jax.sharding import PartitionSpec as P


def from_root(shard, axis, root):
    mine = lax.axis_index(axis) == root
    return lax.psum(jnp.where(mine, shard, jnp.zeros_like(shard)), axis)


def normalize(block, ln_gain, ln_bias):
    values = block.astype(jnp.float32)
    center = jnp.mean(values, axis=-1, keepdims=True)
    spread = jnp.mean((values - center) ** 2, axis=-1, keepdims=True)
    return ((values - center) / jnp.sqrt(spread + 1e-05) * ln_gain + ln_bias).astype(jnp.bfloat16)


def activate(flat, weight, masks, rows, cols):
    chans = weight.shape[1] // 2
    proj = jnp.dot(flat, weight, preferred_element_type=jnp.float32)
    acted = jax.nn.sigmoid(proj[:, :chans]) * proj[:, chans:] * masks.reshape(rows * cols, 1)
    return acted.astype(jnp.bfloat16).T.reshape(chans, rows, cols)


def per_device(pair, token_mask, ln_gain, ln_bias, w_left, w_right, w_gate, w_out):
    rows, cols, width = pair.shape
    row_start = lax.axis_index("row") * rows
    col_start = lax.axis_index("col") * cols
    maskf = token_mask.astype(jnp.float32)
    row_mask = lax.dynamic_slice_in_dim(maskf, row_start, rows, 0)
    col_mask = lax.dynamic_slice_in_dim(maskf, col_start, cols, 0)
    masks = row_mask[:, None] * col_mask[None, :]
    normed = normalize(pair, ln_gain, ln_bias)
    flat = normed.reshape(rows * cols, width)
    left_act = activate(flat, w_left, masks, rows, cols)
    right_act = activate(flat, w_right, masks, rows, cols)
    right_rows = lax.all_gather(right_act, "col", axis=2, tiled=True)
    offset = col_start % rows
    root = col_start // rows
    right_piece = lax.dynamic_slice_in_dim(right_rows, offset, cols, 1)
    right_panel = from_root(right_piece, "row", root)
    tokens_all = right_panel.shape[2]
    scale = 4.0 / math.sqrt(tokens_all)
    left_panel = lax.all_gather(left_act, "col", axis=2, tiled=True)
    total = jnp.einsum("cik,cjk->cij", left_panel, right_panel, preferred_element_type=jnp.float32)
    tri = (scale * total).astype(jnp.bfloat16)
    gate = jax.nn.sigmoid(jnp.dot(flat, w_gate, preferred_element_type=jnp.float32))
    mixed = jnp.einsum("cij,cd->ijd", tri, w_out, preferred_element_type=jnp.float32)
    return (gate.reshape(rows, cols, width) * mixed).astype(jnp.bfloat16)


def solution(mesh):
    placed = (P("row", "col", None), P(), P(), P(), P(), P(), P(), P())
    return jax.shard_map(
        per_device, mesh=mesh, in_specs=placed, out_specs=P("row", "col", None), check_vma=False
    )
```

profile of v0, /device:TPU:1, one launch (start us, length us, event | category | flops | bytes accessed | tf_op | source)
XLA Modules:
  0.0 425.6 jit_solution(5560557466786236299)
XLA Ops:
  6.5 0.0 copy-start
  6.5 0.0 all-gather.5.cloned.1.call-start
  6.5 0.7 convert_element_type.23
  7.2 0.1 dynamic_slice.10
  7.3 0.1 dynamic_slice.9
  7.4 0.1 broadcast_multiply_fusion
  7.5 0.1 mul.71
  7.6 1.2 convert_reduce_fusion
  8.8 1.4 fusion.6
  10.1 1.4 fusion.9
  11.5 0.0 copy-done
  11.5 0.3 fusion.26
  11.8 1.0 fusion.25
  12.9 0.2 fusion.22
  13.0 0.9 copy.10
  13.9 0.0 all-gather.5.cloned.1.call-update
  13.9 0.0 all-gather.3.cloned.1.call-start
  14.0 0.9 copy.9
  14.9 0.0 all-gather.3.cloned.1.call-update
  14.9 0.0 all-reduce.2.cloned.1.call-start
  15.0 82.4 %all-gather.5.cloned.1.call-done = bf16[64,48,768]{0,2,1:T(8,128)(2,1)} async-done(((bf16[64,48,24]{0,2,1:T(8,128)(2,1)}), bf16[64,48,768]{0,2,1:T(8,128)(2,1)}) %all-gather.5.cloned.1.call-update) | async-done | bytes 4718608 | tf_op jit(solution)/shard_map/all_gather | solution.py:40
  97.4 4.8 %dynamic-slice_select_fusion = bf16[64,24,768]{0,2,1:T(8,128)(2,1)} fusion(bf16[64,48,768]{0,2,1:T(8,128)(2,1)} %all-gather.5.cloned.1.call-done, s32[]{:T(128)S(6)} %select_n.33, pred[]{:T(512)S(6)} %eq.5), kind=kLoop, calls=%fused_computation | loop fusion | flops 1179648 | bytes 4718597 | tf_op jit(solution)/shard_map/jit(_where)/select_n | solution.py:11
  102.2 0.0 copy-start.2
  102.2 0.0 all-reduce.2.cloned.1.call-update
  102.2 0.7 copy-done.2
  103.0 1.1 fusion.2
  104.1 72.2 %all-gather.3.cloned.1.call-done = bf16[64,48,768]{0,2,1:T(8,128)(2,1)} async-done(((bf16[64,48,24]{0,2,1:T(8,128)(2,1)}), bf16[64,48,768]{0,2,1:T(8,128)(2,1)}) %all-gather.3.cloned.1.call-update) | async-done | bytes 4718608 | tf_op jit(solution)/shard_map/all_gather | solution.py:47
  176.3 11.5 %copy.11 = bf16[64,48,768]{2,1,0:T(8,128)(2,1)} copy(bf16[64,48,768]{0,2,1:T(8,128)(2,1)} %all-gather.3.cloned.1.call-done) | data formatting | bytes 9437184 | tf_op jit(solution)/shard_map/all_gather | solution.py:47
  187.8 220.1 %all-reduce.2.cloned.1.call-done = bf16[64,24,768]{0,2,1:T(8,128)(2,1)} async-done(((bf16[64,24,768]{0,2,1:T(8,128)(2,1)}), bf16[64,24,768]{0,2,1:T(8,128)(2,1)}) %all-reduce.2.cloned.1.call-update) | async-done | bytes 2359312 | tf_op jit(solution)/shard_map/psum | solution.py:11
  407.9 5.1 %copy.12 = bf16[64,24,768]{2,1,0:T(8,128)(2,1)S(1)} copy(bf16[64,24,768]{0,2,1:T(8,128)(2,1)} %all-reduce.2.cloned.1.call-done) | data formatting | bytes 4718592 | tf_op jit(solution)/shard_map/psum | solution.py:11
  412.9 0.0 copy-start.1
  412.9 3.7 fusion.27
  416.6 0.3 copy.13
  417.0 0.0 copy-done.1
  417.0 2.1 fusion.3
  (2 shorter events, 0.0 us)
Async XLA Ops:
  6.5 5.0 %copy-start = (bf16[128,128]{1,0:T(8,128)(2,1)S(1)}, bf16[128,128]{1,0:T(8,128)(2,1)}, u32[]{:S(2)}) copy-start(bf16[128,128]{1,0:T(8,128)(2,1)} %param.13) | copy-start | bytes 98308
  6.5 90.9 %all-gather.5.cloned.1.call-start = ((), (), s32[]{:S(2)}) async-start(), calls=%async_computation.1 | async-start | bytes 9732096 | tf_op jit(solution)/shard_map/all_gather | solution.py:40
  13.9 162.4 %all-gather.3.cloned.1.call-start = ((), (), s32[]{:S(2)}) async-start(), calls=%async_computation | async-start | bytes 9732096 | tf_op jit(solution)/shard_map/all_gather | solution.py:47
  14.9 392.9 %all-reduce.2.cloned.1.call-start = ((), (), s32[]{:S(2)}) async-start(), calls=%async_computation.2 | async-start | bytes 9437184 | tf_op jit(solution)/shard_map/psum | solution.py:11
  102.2 0.8 copy-start.2
  412.9 4.0 copy-start.1
Sparse Core Ops, SparseCore 0:
  14.1 83.2 all-gather.4
  99.5 76.8 all-gather.2
  179.3 228.5 all-reduce.1
where the time goes:
time: 428 us; the launch traced here: 426 us
  waiting for transfers between devices  375 us (88%)
  local copies, waits for them, and re-layouts  19.6 us (5%)
  between operations  13.3 us (3%)
  other arithmetic  9.67 us (2%)
  matrix products  8.21 us (2%)
    psum x1, waiting for transfers between devices, from_root(): return lax.psum(jnp.where(mine, shard, jnp.zeros_like(shard)), axis)  220 us
    all_gather x1, waiting for transfers between devices, per_device(): right_rows = lax.all_gather(right_act, 'col', axis=2, tiled=True)  82.4 us
    all_gather x1, waiting for transfers between devices, per_device(): left_panel = lax.all_gather(left_act, 'col', axis=2, tiled=True)  72.2 us
    all_gather x1, local copies, waits for them, and re-layouts, per_device(): left_panel = lax.all_gather(left_act, 'col', axis=2, tiled=True)  11.5 us
  transfers between devices with their start and end apart: 3, of which 3 were waited for; matrix products, arithmetic and copies ran while one was open for 4% of the time, Pallas kernels for 0%

commit v1 on v0

v1 whole, which is shorter than its diff:
```python
import functools
import math

import jax
import jax.numpy as jnp
from jax import lax
from jax.experimental import pallas as pl
from jax.experimental.pallas import tpu as pltpu
from jax.sharding import PartitionSpec as P

F32 = jnp.float32
BF16 = jnp.bfloat16
MESH = pl.DeviceIdType.MESH


def one_hot(shape, source):
    row = lax.broadcasted_iota(jnp.int32, shape, 0)
    col = lax.broadcasted_iota(jnp.int32, shape, 1)
    return row, col, source(row)


def permutation(count, source):
    _, col, src = one_hot((count, count), source)
    return jnp.where(col == src, 1.0, 0.0).astype(BF16)


def swap_ends(a, b, c):
    return permutation(a * b * c, lambda o: (o % a) * (b * c) + ((o // a) % b) * c + o // (a * b))


def nt_dot(x, y):
    return lax.dot_general(x, y, (((1,), (1,)), ((), ())), preferred_element_type=F32)


def tn_dot(x, y):
    return lax.dot_general(x, y, (((0,), (0,)), ((), ())), preferred_element_type=F32)


def nn_dot(x, y):
    return lax.dot_general(x, y, (((1,), (0,)), ((), ())), preferred_element_type=F32)


def exchange(parts, width):
    n = len(parts)
    total = n * width
    pos = lax.broadcasted_iota(jnp.int32, parts[0].shape, 1) // width
    rolled = [parts[0]] + [pltpu.roll(parts[y], y * width, 1) for y in range(1, n)]
    result = []
    for k in range(n):
        picked = rolled[0]
        for y in range(1, n):
            picked = jnp.where(pos == (k + y) % n, rolled[y], picked)
        result.append(picked if k == 0 else pltpu.roll(picked, total - k * width, 1))
    return result


def fold(block):
    third = block.shape[1] // 3
    a, b, c = (block[:, i * third:(i + 1) * third] for i in range(3))
    return jnp.concatenate(
        [jnp.concatenate([a, b], 0), jnp.concatenate([c, jnp.zeros_like(c)], 0)], 1
    )


def unfold(block):
    n, third = block.shape[0] // 2, block.shape[1] // 2
    return jnp.concatenate([block[:n, :third], block[n:, :third], block[:n, third:]], 1)


def kernel(
    ny, nz, tm, pair, gain, bias, w_left, w_right, w_gate, w_out, out,
    n32, normed, gate, wt, a1, b1, a2, b2, lx, rs, rx, pp, qq, sa, fa, ga, ha, sb, fb, gb, hb,
    s1, r1, s2, r2, sl, rl, sr, rr, sq, rq, s3, r3, s4, r4,
):
    rows, cols, width = pair.shape
    nt = cols // ny
    lanes = ny * rows
    chans = ny * nz
    row, col = lax.axis_index("row"), lax.axis_index("col")
    y, xh = row // 2, row % 2
    z, xl, core = col // 4, (col // 2) % 2, col % 2
    same = xl == xh

    def at_y(d):
        return lax.rem(y + d, ny)

    def at_z(d):
        return lax.rem(z + d, nz)

    def dev_y(other):
        return (other * 2 + xh, col)

    def dev_z(other):
        return (row, other * 4 + xl * 2 + core)

    def dev_x(oh, ol):
        return (y * 2 + oh, z * 4 + ol * 2 + core)

    other_core = (row, z * 4 + xl * 2 + 1 - core)
    peers = [dev_y(at_y(d)) for d in range(1, ny)] + [dev_z(at_z(d)) for d in range(1, nz)]
    peers += [dev_x(xh, 1 - xl), dev_x(1 - xh, xl), dev_x(1 - xh, 1 - xl), other_core]
    barrier = pltpu.get_barrier_semaphore()
    for peer in peers:
        pl.semaphore_signal(barrier, inc=1, device_id=peer, device_id_type=MESH)

    def send(src, dst, send_sem, recv_sem, device):
        pltpu.make_async_remote_copy(
            src_ref=src, dst_ref=dst, send_sem=send_sem, recv_sem=recv_sem,
            device_id=device, device_id_type=MESH,
        ).start()

    def take(ref, sem):
        pltpu.make_async_copy(ref, ref, sem).wait()

    def weight_rows(offset):
        total = None
        for side, weight in ((0, w_left), (1, w_right)):
            r, c, src = one_hot(
                (2 * chans, 2 * chans), lambda o: (o // (2 * nz)) * nz + o % nz + offset
            )
            pick = jnp.where((c == src) & ((r // nz) % 2 == side), 1.0, 0.0).astype(BF16)
            part = nt_dot(pick, weight[...])
            total = part if total is None else total + part
        return total.astype(BF16)

    wt[0:2 * chans, :] = weight_rows(0)
    wt[2 * chans:4 * chans, :] = weight_rows(chans)

    lane = lax.broadcasted_iota(jnp.int32, (1, lanes), 1)
    row_mask = jnp.zeros((1, lanes), F32)
    for i in range(rows):
        row_mask = jnp.where(lane % rows == i, tm[row * rows + i].astype(F32), row_mask)

    def mask_of(t):
        col_mask = jnp.zeros((1, lanes), F32)
        for k in range(ny):
            col_mask = jnp.where(lane // rows == k, tm[col * cols + t * ny + k].astype(F32), col_mask)
        return row_mask * col_mask

    def project(t):
        block = pair[:, t * ny:(t + 1) * ny, :].astype(F32)
        center = jnp.mean(block, axis=-1, keepdims=True)
        delta = block - center
        spread = jnp.mean(delta * delta, axis=-1, keepdims=True)
        value = delta * lax.rsqrt(spread + 1e-05) * gain[...].reshape(1, 1, width) + bias[...].reshape(1, 1, width)
        n32[t] = value.reshape(rows * ny, width)
        for k in range(ny):
            normed[t, k * rows:(k + 1) * rows, :] = n32[t, pl.ds(k, rows, stride=ny), :].astype(BF16)
        proj = nt_dot(wt[...], normed[t])
        act = jax.nn.sigmoid(proj[:2 * chans]) * proj[2 * chans:] * mask_of(t)
        a1[t] = act.astype(BF16).reshape(ny, 2 * nz, lanes)

    def send_y(t):
        for d in range(1, ny):
            to = at_y(d)
            send(a1.at[t, to], b1.at[t, y], s1.at[t], r1.at[t], dev_y(to))
        b1[t, y] = a1[t, y]

    swap1 = swap_ends(ny, 2, nz)

    def turn(t):
        take(b1.at[t, pl.ds(0, ny - 1)], r1.at[t])
        parts = exchange([b1[t, k].astype(F32) for k in range(ny)], rows)
        stacked = jnp.concatenate(parts, 0).astype(BF16)
        a2[t] = nn_dot(swap1, stacked).astype(BF16).reshape(nz, 2 * ny, lanes)
        for d in range(1, nz):
            to = at_z(d)
            send(a2.at[t, to], b2.at[t, z], s2.at[t], r2.at[t], dev_z(to))
        b2[t, z] = a2[t, z]

    def spread_x(t):
        take(b2.at[t, pl.ds(0, nz - 1)], r2.at[t])
        both = b2[t].astype(F32).reshape(nz, 2, ny, lanes)
        lx[xl, t] = both[:, 0].reshape(nz * ny, lanes).astype(BF16)
        send(lx.at[xl, t], lx.at[xl, t], sl.at[t], rl.at[t], dev_x(xh, 1 - xl))
        right = both[:, 1].reshape(nz * ny, lanes).astype(BF16)
        rs[t] = right
        send(rs.at[t], rx.at[xl, t], sr.at[t], rr.at[t], dev_x(1 - xh, xh))

        @pl.when(same)
        def _():
            rx[xl, t] = right

        @pl.when(jnp.logical_not(same))
        def _():
            send(rs.at[t], rx.at[xl, t], sr.at[t], rr.at[t], dev_x(xh, xh))

    def gather_x(t):
        take(lx.at[0, t], rl.at[t])

        @pl.when(same)
        def _():
            take(rx.at[0, t], rr.at[t])

        @pl.when(jnp.logical_not(same))
        def _():
            take(rx.at[:, t], rr.at[t])

    project(0)
    pl.semaphore_wait(barrier, len(peers))
    send_y(0)
    for t in range(1, nt):
        project(t)
        send_y(t)
    turn(0)
    turn(1)
    spread_x(0)
    turn(2)
    spread_x(1)
    for t in range(nt):
        gate[t] = jax.nn.sigmoid(nn_dot(normed[t], w_gate[...]))
    spread_x(2)

    half = nz * ny * 2
    gather_x(0)
    gather_x(1)
    first = tn_dot(rx[:, 0:2].reshape(2 * half, lanes), lx[:, 0:2].reshape(2 * half, lanes))
    gather_x(2)
    total = first + tn_dot(rx[:, 2].reshape(half, lanes), lx[:, 2].reshape(half, lanes))
    pp[...] = total.reshape(nz, rows, lanes)
    send(pp.at[:, pl.ds((1 - core) * cols, cols), :], qq, sq, rq, other_core)
    take(qq, rq)
    scale = 4.0 / math.sqrt(rows * 2 * ny)
    two = 2 * ny

    tri = (pp[:, pl.ds(core * cols, cols), :] + qq[...]) * scale
    sa[...] = tri[:, :two].astype(BF16)
    for d in range(1, nz):
        to = at_z(d)
        send(sa.at[to], fa.at[z], s3.at[0], r3.at[0], dev_z(to))
    for k in range(nz):
        sb[k] = fold(tri[k, two:]).astype(BF16)
    for d in range(1, nz):
        to = at_z(d)
        send(sb.at[to], fb.at[z], s3.at[1], r3.at[1], dev_z(to))
    fa[z] = sa[z]
    fb[z] = sb[z]

    take(fa.at[pl.ds(0, nz - 1)], r3.at[0])
    turned = nn_dot(swap_ends(nz, 2, ny), fa[...].reshape(nz * two, lanes)).reshape(ny, 2 * nz, lanes)
    parts = exchange([turned[j] for j in range(ny)], rows)
    for k in range(ny):
        ga[k] = parts[k].astype(BF16)
    for d in range(1, ny):
        to = at_y(d)
        send(ga.at[to], ha.at[y], s4.at[0], r4.at[0], dev_y(to))
    ha[y] = ga[y]

    take(fb.at[pl.ds(0, nz - 1)], r3.at[1])
    flat = jnp.concatenate([unfold(fb[k].astype(F32)) for k in range(nz)], 0).astype(BF16)
    turned = nn_dot(swap_ends(nz, 1, ny), flat).reshape(ny, nz, lanes)
    parts = exchange([turned[j] for j in range(ny)], rows)
    for k in range(ny):
        gb[k] = fold(parts[k]).astype(BF16)
    for d in range(1, ny):
        to = at_y(d)
        send(gb.at[to], hb.at[y], s4.at[1], r4.at[1], dev_y(to))
    hb[y] = gb[y]

    def finish(t, block):
        mixed = tn_dot(block.reshape(chans, lanes).astype(BF16), w_out[...])
        out[t * ny:(t + 1) * ny] = (gate[t] * mixed).astype(BF16).reshape(ny, rows, width)

    take(ha.at[pl.ds(0, ny - 1)], r4.at[0])
    both = ha[...].astype(F32).reshape(ny, 2, nz, lanes)
    finish(0, both[:, 0])
    finish(1, both[:, 1])
    take(hb.at[pl.ds(0, ny - 1)], r4.at[1])
    finish(2, jnp.concatenate([unfold(hb[k].astype(F32)) for k in range(ny)], 0))

    for t in range(nt):
        take(a1.at[t, pl.ds(0, ny - 1)], s1.at[t])
        take(a2.at[t, pl.ds(0, nz - 1)], s2.at[t])
        take(lx.at[0, t], sl.at[t])

        @pl.when(same)
        def _():
            take(rx.at[0, t], sr.at[t])

        @pl.when(jnp.logical_not(same))
        def _():
            take(rx.at[:, t], sr.at[t])
    take(qq, sq)
    take(sa.at[pl.ds(0, nz - 1)], s3.at[0])
    take(sb.at[pl.ds(0, nz - 1)], s3.at[1])
    take(ga.at[pl.ds(0, ny - 1)], s4.at[0])
    take(gb.at[pl.ds(0, ny - 1)], s4.at[1])


def per_device(ny, nz, pair, token_mask, ln_gain, ln_bias, w_left, w_right, w_gate, w_out):
    rows, cols, width = pair.shape
    lanes = ny * rows
    nt = cols // ny
    chans = ny * nz
    third = 2 * lanes // 3
    dma = pltpu.SemaphoreType.DMA
    vmem = pl.BlockSpec(memory_space=pltpu.VMEM)
    swapped = pl.pallas_call(
        functools.partial(kernel, ny, nz),
        out_shape=jax.ShapeDtypeStruct((cols, rows, width), BF16),
        in_specs=[pl.BlockSpec(memory_space=pltpu.SMEM)] + [vmem] * 7,
        out_specs=vmem,
        scratch_shapes=[
            pltpu.VMEM((nt, rows * ny, width), F32),
            pltpu.VMEM((nt, rows * ny, width), BF16),
            pltpu.VMEM((nt, rows * ny, width), F32),
            pltpu.VMEM((4 * chans, width), BF16),
            pltpu.VMEM((nt, ny, 2 * nz, lanes), BF16),
            pltpu.VMEM((nt, ny, 2 * nz, lanes), BF16),
            pltpu.VMEM((nt, nz, 2 * ny, lanes), BF16),
            pltpu.VMEM((nt, nz, 2 * ny, lanes), BF16),
            pltpu.VMEM((2, nt, nz * ny, lanes), BF16),
            pltpu.VMEM((nt, nz * ny, lanes), BF16),
            pltpu.VMEM((2, nt, nz * ny, lanes), BF16),
            pltpu.VMEM((nz, rows, lanes), F32),
            pltpu.VMEM((nz, cols, lanes), F32),
            pltpu.VMEM((nz, 2 * ny, lanes), BF16),
            pltpu.VMEM((nz, 2 * ny, lanes), BF16),
            pltpu.VMEM((ny, 2 * nz, lanes), BF16),
            pltpu.VMEM((ny, 2 * nz, lanes), BF16),
            pltpu.VMEM((nz, 2 * ny, third), BF16),
            pltpu.VMEM((nz, 2 * ny, third), BF16),
            pltpu.VMEM((ny, 2 * nz, third), BF16),
            pltpu.VMEM((ny, 2 * nz, third), BF16),
        ] + [dma((nt,))] * 8 + [dma, dma] + [dma((2,))] * 4,
        compiler_params=pltpu.CompilerParams(
            collective_id=0, has_side_effects=True, vmem_limit_bytes=48 * 1024 * 1024
        ),
    )(token_mask, pair, ln_gain.reshape(1, width), ln_bias.reshape(1, width), w_left, w_right, w_gate, w_out)
    return jnp.transpose(swapped, (1, 0, 2))


def solution(mesh):
    ny, nz = mesh.shape["row"] // 2, mesh.shape["col"] // 4
    placed = (P("row", "col", None), P(), P(), P(), P(), P(), P(), P())
    return jax.shard_map(
        functools.partial(per_device, ny, nz), mesh=mesh, in_specs=placed,
        out_specs=P("row", "col", None), check_vma=False,
    )
```

time: 428 us -> 59.1 us (0.14)
  waiting for transfers between devices: 375 us -> 0 us
  Pallas kernels: 0 us -> 52.5 us
  local copies, waits for them, and re-layouts: 19.6 us -> 6.1 us
  between operations: 13.3 us -> 0.02 us
  other arithmetic: 9.67 us -> 0 us
  matrix products: 8.21 us -> 0 us
    psum x1 -> x0, waiting for transfers between devices: 220 us -> none  [from_root(): return lax.psum(jnp.where(mine, shard, jnp.zeros_like(shard)), axis)]
    all_gather x2 -> x0, waiting for transfers between devices: 155 us -> none  [the longest x1 82.4 us: per_device(): right_rows = lax.all_gather(right_act, 'col', axis=2, tiled=True)]
    pallas_call x0 -> x1, Pallas kernels: none -> 52.5 us  [per_device(): pl.pallas_call(functools.partial(kernel, ny, nz), out_shape=jax.ShapeDtyp...]
    all_gather x1 -> x0, local copies, waits for them, and re-layouts: 11.5 us -> none  [per_device(): left_panel = lax.all_gather(left_act, 'col', axis=2, tiled=True)]
    dot_general x5 -> x0, matrix products: 8.21 us -> none  [the longest x1 3.68 us: per_device(): jnp.einsum('cik,cjk->cij', left_panel, right_panel, preferred_element_typ...]
    psum x1 -> x0, local copies, waits for them, and re-layouts: 5.05 us -> none  [from_root(): return lax.psum(jnp.where(mine, shard, jnp.zeros_like(shard)), axis)]
    select_n x1 -> x0, other arithmetic: 4.81 us -> none  [from_root(): return lax.psum(jnp.where(mine, shard, jnp.zeros_like(shard)), axis)]
    unnamed x6 -> x16, local copies, waits for them, and re-layouts: 0.74 us -> 5.31 us
  transfers between devices with their start and end apart: 3 -> 0, of which waited for: 3 -> 0; matrix products, arithmetic and copies ran while one was open for 4% -> 0% of each run, Pallas kernels for 0% -> 0%
where the time goes in v1:
time: 59.1 us; the launch traced here: 58.6 us
  Pallas kernels  52.5 us (89%)
  local copies, waits for them, and re-layouts  6.1 us (10%)
    pallas_call x1, Pallas kernels, per_device(): pl.pallas_call(functools.partial(kernel, ny, nz), out_shape=jax.ShapeDtyp...  52.5 us
    unnamed x16, local copies, waits for them, and re-layouts  5.31 us

profile of v1, /device:TPU:1, one launch (start us, length us, event | category | flops | bytes accessed | tf_op | source)
XLA Modules:
  0.0 58.6 jit_solution(13051801956374459729)
XLA Ops:
  0.0 0.0 copy-start.6
  0.0 0.0 copy-start.7
  0.0 0.7 %copy-done.6 = f32[128]{0:T(128)S(1)} copy-done((f32[128]{0:T(128)S(1)}, f32[128]{0:T(128)}, u32[]{:S(2)}) %copy-start.6) | copy-done | bytes 536
  0.7 0.0 copy-done.7
  0.7 0.0 copy-start
  0.7 1.0 %copy-done = bf16[48,24,128]{2,1,0:T(8,128)(2,1)S(1)} copy-done((bf16[48,24,128]{2,1,0:T(8,128)(2,1)S(1)}, bf16[48,24,128]{2,1,0:T(8,128)(2,1)}, u32[]{:S(2)}) %copy-start) | copy-done | bytes 294936
  1.6 0.0 copy-start.1
  1.6 0.8 %copy-done.1 = bf16[128,128]{1,0:T(8,128)(2,1)S(1)} copy-done((bf16[128,128]{1,0:T(8,128)(2,1)S(1)}, bf16[128,128]{1,0:T(8,128)(2,1)}, u32[]{:S(2)}) %copy-start.1) | copy-done | bytes 32792
  2.4 0.0 copy-start.2
  2.4 0.8 %copy-done.2 = bf16[128,128]{1,0:T(8,128)(2,1)S(1)} copy-done((bf16[128,128]{1,0:T(8,128)(2,1)S(1)}, bf16[128,128]{1,0:T(8,128)(2,1)}, u32[]{:S(2)}) %copy-start.2) | copy-done | bytes 32792
  3.2 0.0 copy-start.3
  3.2 0.8 %copy-done.3 = bf16[128,128]{1,0:T(8,128)(2,1)S(1)} copy-done((bf16[128,128]{1,0:T(8,128)(2,1)S(1)}, bf16[128,128]{1,0:T(8,128)(2,1)}, u32[]{:S(2)}) %copy-start.3) | copy-done | bytes 32792
  3.9 0.0 copy-start.4
  3.9 0.7 %copy-done.4 = bf16[64,128]{1,0:T(8,128)(2,1)S(1)} copy-done((bf16[64,128]{1,0:T(8,128)(2,1)S(1)}, bf16[64,128]{1,0:T(8,128)(2,1)}, u32[]{:S(2)}) %copy-start.4) | copy-done | bytes 16408
  4.6 0.0 copy-start.5
  4.6 0.7 %copy-done.5 = s32[768]{0:T(1024)S(1)} copy-done((s32[768]{0:T(1024)S(1)}, s32[768]{0:T(1024)}, u32[]{:S(2)}) %copy-start.5) | copy-done | bytes 3096
  5.3 52.5 %shard_map.82 = bf16[24,48,128]{2,1,0:T(8,128)(2,1)S(1)} custom-call(s32[768]{0:T(1024)S(1)} %copy-done.5, bf16[48,24,128]{2,1,0:T(8,128)(2,1)S(1)} %copy-done, f32[1,128]{1,0:T(1,128)S(1)} %bitcast.4, f32[1,128]{1,0:T(1,128)S(1)} %bitcast.5, bf16[128,128]{1,0:T(8,128)(2,1)S(1)} %copy-done.1, bf16[128,128]{1,0:T(8,128)(2,1)S(1)} %copy-done.2, ...), custom_call_target="tpu_custom_call" | custom-call | tf_op jit(solution)/shard_map/pallas_call | solution.py:298
  57.8 0.8 %copy.9 = bf16[48,24,128]{2,1,0:T(8,128)(2,1)} copy(bf16[48,24,128]{2,0,1:T(8,128)(2,1)S(1)} %bitcast.3) | data formatting | bytes 589824 | tf_op jit(solution)/shard_map/transpose | solution.py:330
Async XLA Ops:
  0.0 0.7 %copy-start.6 = (f32[128]{0:T(128)S(1)}, f32[128]{0:T(128)}, u32[]{:S(2)}) copy-start(f32[128]{0:T(128)} %param.10) | copy-start | bytes 1540
  0.0 0.7 %copy-start.7 = (f32[128]{0:T(128)S(1)}, f32[128]{0:T(128)}, u32[]{:S(2)}) copy-start(f32[128]{0:T(128)} %param.11) | copy-start | bytes 1540
  0.7 1.0 %copy-start = (bf16[48,24,128]{2,1,0:T(8,128)(2,1)S(1)}, bf16[48,24,128]{2,1,0:T(8,128)(2,1)}, u32[]{:S(2)}) copy-start(bf16[48,24,128]{2,1,0:T(8,128)(2,1)} %pair.1) | copy-start | bytes 884740
  1.6 0.8 %copy-start.1 = (bf16[128,128]{1,0:T(8,128)(2,1)S(1)}, bf16[128,128]{1,0:T(8,128)(2,1)}, u32[]{:S(2)}) copy-start(bf16[128,128]{1,0:T(8,128)(2,1)} %w_left.1) | copy-start | bytes 98308
  2.4 0.8 %copy-start.2 = (bf16[128,128]{1,0:T(8,128)(2,1)S(1)}, bf16[128,128]{1,0:T(8,128)(2,1)}, u32[]{:S(2)}) copy-start(bf16[128,128]{1,0:T(8,128)(2,1)} %w_right.1) | copy-start | bytes 98308
  3.2 0.8 %copy-start.3 = (bf16[128,128]{1,0:T(8,128)(2,1)S(1)}, bf16[128,128]{1,0:T(8,128)(2,1)}, u32[]{:S(2)}) copy-start(bf16[128,128]{1,0:T(8,128)(2,1)} %w_gate.1) | copy-start | bytes 98308
  3.9 0.7 %copy-start.4 = (bf16[64,128]{1,0:T(8,128)(2,1)S(1)}, bf16[64,128]{1,0:T(8,128)(2,1)}, u32[]{:S(2)}) copy-start(bf16[64,128]{1,0:T(8,128)(2,1)} %w_out.1) | copy-start | bytes 49156
  4.6 0.7 %copy-start.5 = (s32[768]{0:T(1024)S(1)}, s32[768]{0:T(1024)}, u32[]{:S(2)}) copy-start(s32[768]{0:T(1024)} %tm.1) | copy-start | bytes 9220

commit v2 on v1

--- a/solution.py
+++ b/solution.py
@@ -26,6 +26,10 @@
 
 def swap_ends(a, b, c):
     return permutation(a * b * c, lambda o: (o % a) * (b * c) + ((o // a) % b) * c + o // (a * b))
+
+
+def far_first(n):
+    return sorted(range(1, n), key=lambda d: -min(d, n - d))
 
 
 def nt_dot(x, y):
@@ -68,14 +72,21 @@
 
 
 def kernel(
-    ny, nz, tm, pair, gain, bias, w_left, w_right, w_gate, w_out, out,
-    n32, normed, gate, wt, a1, b1, a2, b2, lx, rs, rx, pp, qq, sa, fa, ga, ha, sb, fb, gb, hb,
+    ny, nz, tm_hbm, pair_hbm, gain_hbm, bias_hbm, wl_hbm, wr_hbm, wg_hbm, wo_hbm, out,
+    tm, pair, gain, bias, w_left, w_right, w_gate, w_out, load, n32, normed, gate, wt, a1, b1, a2, b2, lx, rs, rx, pp, qq, sa, fa, ga, ha, sb, fb, gb, hb,
     s1, r1, s2, r2, sl, rl, sr, rr, sq, rq, s3, r3, s4, r4,
 ):
     rows, cols, width = pair.shape
     nt = cols // ny
     lanes = ny * rows
     chans = ny * nz
+    loads = [
+        pltpu.make_async_copy(src, dst, load.at[i])
+        for i, (src, dst) in enumerate((
+            (pair_hbm, pair), (wl_hbm, w_left), (wr_hbm, w_right), (tm_hbm, tm),
+            (gain_hbm, gain), (bias_hbm, bias), (wg_hbm, w_gate), (wo_hbm, w_out),
+        ))
+    ]
     row, col = lax.axis_index("row"), lax.axis_index("col")
     y, xh = row // 2, row % 2
     z, xl, core = col // 4, (col // 2) % 2, col % 2
@@ -103,6 +114,9 @@
     for peer in peers:
         pl.semaphore_signal(barrier, inc=1, device_id=peer, device_id_type=MESH)
 
+    for copy in loads:
+        copy.start()
+
     def send(src, dst, send_sem, recv_sem, device):
         pltpu.make_async_remote_copy(
             src_ref=src, dst_ref=dst, send_sem=send_sem, recv_sem=recv_sem,
@@ -111,6 +125,9 @@
 
     def take(ref, sem):
         pltpu.make_async_copy(ref, ref, sem).wait()
+
+    for copy in loads[1:]:
+        copy.wait()
 
     def weight_rows(offset):
         total = None
@@ -151,7 +168,7 @@
         a1[t] = act.astype(BF16).reshape(ny, 2 * nz, lanes)
 
     def send_y(t):
-        for d in range(1, ny):
+        for d in far_first(ny):
             to = at_y(d)
             send(a1.at[t, to], b1.at[t, y], s1.at[t], r1.at[t], dev_y(to))
         b1[t, y] = a1[t, y]
@@ -163,7 +180,7 @@
         parts = exchange([b1[t, k].astype(F32) for k in range(ny)], rows)
         stacked = jnp.concatenate(parts, 0).astype(BF16)
         a2[t] = nn_dot(swap1, stacked).astype(BF16).reshape(nz, 2 * ny, lanes)
-        for d in range(1, nz):
+        for d in far_first(nz):
             to = at_z(d)
             send(a2.at[t, to], b2.at[t, z], s2.at[t], r2.at[t], dev_z(to))
         b2[t, z] = a2[t, z]
@@ -196,6 +213,7 @@
         def _():
             take(rx.at[:, t], rr.at[t])
 
+    loads[0].wait()
     project(0)
     pl.semaphore_wait(barrier, len(peers))
     send_y(0)
@@ -225,12 +243,12 @@
 
     tri = (pp[:, pl.ds(core * cols, cols), :] + qq[...]) * scale
     sa[...] = tri[:, :two].astype(BF16)
-    for d in range(1, nz):
+    for d in far_first(nz):
         to = at_z(d)
         send(sa.at[to], fa.at[z], s3.at[0], r3.at[0], dev_z(to))
     for k in range(nz):
         sb[k] = fold(tri[k, two:]).astype(BF16)
-    for d in range(1, nz):
+    for d in far_first(nz):
         to = at_z(d)
         send(sb.at[to], fb.at[z], s3.at[1], r3.at[1], dev_z(to))
     fa[z] = sa[z]
@@ -241,7 +259,7 @@
     parts = exchange([turned[j] for j in range(ny)], rows)
     for k in range(ny):
         ga[k] = parts[k].astype(BF16)
-    for d in range(1, ny):
+    for d in far_first(ny):
         to = at_y(d)
         send(ga.at[to], ha.at[y], s4.at[0], r4.at[0], dev_y(to))
     ha[y] = ga[y]
@@ -252,7 +270,7 @@
     parts = exchange([turned[j] for j in range(ny)], rows)
     for k in range(ny):
         gb[k] = fold(parts[k]).astype(BF16)
-    for d in range(1, ny):
+    for d in far_first(ny):
         to = at_y(d)
         send(gb.at[to], hb.at[y], s4.at[1], r4.at[1], dev_y(to))
     hb[y] = gb[y]
@@ -294,13 +312,21 @@
     chans = ny * nz
     third = 2 * lanes // 3
     dma = pltpu.SemaphoreType.DMA
-    vmem = pl.BlockSpec(memory_space=pltpu.VMEM)
     swapped = pl.pallas_call(
         functools.partial(kernel, ny, nz),
         out_shape=jax.ShapeDtypeStruct((cols, rows, width), BF16),
-        in_specs=[pl.BlockSpec(memory_space=pltpu.SMEM)] + [vmem] * 7,
-        out_specs=vmem,
+        in_specs=[pl.BlockSpec(memory_space=pl.ANY)] * 8,
+        out_specs=pl.BlockSpec(memory_space=pltpu.VMEM),
         scratch_shapes=[
+            pltpu.SMEM(token_mask.shape, jnp.int32),
+            pltpu.VMEM(pair.shape, BF16),
+            pltpu.VMEM((1, width), F32),
+            pltpu.VMEM((1, width), F32),
+            pltpu.VMEM(w_left.shape, BF16),
+            pltpu.VMEM(w_right.shape, BF16),
+            pltpu.VMEM(w_gate.shape, BF16),
+            pltpu.VMEM(w_out.shape, BF16),
+            dma((8,)),
             pltpu.VMEM((nt, rows * ny, width), F32),
             pltpu.VMEM((nt, rows * ny, width), BF16),
             pltpu.VMEM((nt, rows * ny, width), F32),
@@ -324,7 +350,7 @@
             pltpu.VMEM((ny, 2 * nz, third), BF16),
         ] + [dma((nt,))] * 8 + [dma, dma] + [dma((2,))] * 4,
         compiler_params=pltpu.CompilerParams(
-            collective_id=0, has_side_effects=True, vmem_limit_bytes=48 * 1024 * 1024
+            collective_id=0, has_side_effects=True, vmem_limit_bytes=64 * 1024 * 1024
         ),
     )(token_mask, pair, ln_gain.reshape(1, width), ln_bias.reshape(1, width), w_left, w_right, w_gate, w_out)
     return jnp.transpose(swapped, (1, 0, 2))

time: 59.1 us -> 50.9 us (0.86)
  local copies, waits for them, and re-layouts: 6.1 us -> 1.75 us
  Pallas kernels: 52.5 us -> 49 us
    unnamed x16 -> x0, local copies, waits for them, and re-layouts: 5.31 us -> none
    pallas_call x1, Pallas kernels: 52.5 us -> 49 us  [per_device(): pl.pallas_call(functools.partial(kernel, ny, nz), out_shape=jax.ShapeDtyp...]
    transpose x1, local copies, waits for them, and re-layouts: 0.79 us -> 1.75 us  [per_device(): return jnp.transpose(swapped, (1, 0, 2))]
where the time goes in v2:
time: 50.9 us; the launch traced here: 50.7 us
  Pallas kernels  49 us (96%)
  local copies, waits for them, and re-layouts  1.75 us (3%)
    pallas_call x1, Pallas kernels, per_device(): pl.pallas_call(functools.partial(kernel, ny, nz), out_shape=jax.ShapeDtyp...  49 us
    transpose x1, local copies, waits for them, and re-layouts, per_device(): return jnp.transpose(swapped, (1, 0, 2))  1.75 us

profile of v2, /device:TPU:1, one launch (start us, length us, event | category | flops | bytes accessed | tf_op | source)
XLA Modules:
  0.0 50.7 jit_solution(3341317501208643450)
XLA Ops:
  0.0 49.0 %shard_map.82 = bf16[24,48,128]{2,1,0:T(8,128)(2,1)} custom-call(s32[768]{0:T(1024)} %tm_hbm.1, bf16[48,24,128]{2,1,0:T(8,128)(2,1)} %pair_hbm.1, f32[1,128]{1,0:T(1,128)} %bitcast.4, f32[1,128]{1,0:T(1,128)} %bitcast.5, bf16[128,128]{1,0:T(8,128)(2,1)} %wl_hbm.1, bf16[128,128]{1,0:T(8,128)(2,1)} %wr_hbm.1, bf16[128,128]{1,0:T(8,128)(2,1)} %wg_hbm.1, ...), custom_call_target="tpu_custom_call" | custom-call | tf_op jit(solution)/shard_map/pallas_call | solution.py:315
  49.0 1.8 %copy.9 = bf16[48,24,128]{2,1,0:T(8,128)(2,1)} copy(bf16[48,24,128]{2,0,1:T(8,128)(2,1)} %bitcast.3) | data formatting | bytes 589824 | tf_op jit(solution)/shard_map/transpose | solution.py:356

commit v3 on v2

--- a/solution.py
+++ b/solution.py
@@ -73,8 +73,10 @@
 
 def kernel(
     ny, nz, tm_hbm, pair_hbm, gain_hbm, bias_hbm, wl_hbm, wr_hbm, wg_hbm, wo_hbm, out,
-    tm, pair, gain, bias, w_left, w_right, w_gate, w_out, load, n32, normed, gate, wt, a1, b1, a2, b2, lx, rs, rx, pp, qq, sa, fa, ga, ha, sb, fb, gb, hb,
-    s1, r1, s2, r2, sl, rl, sr, rr, sq, rq, s3, r3, s4, r4,
+    tm, pair, gain, bias, w_left, w_right, w_gate, w_out, load, n32, normed, gate, wt,
+    a1l, a1lf, b1l, b1lf, a1r, a1rf, b1r, b1rf, a2l, a2lf, b2l, b2lf, a2r, a2rf, b2r, b2rf, rx, rxf,
+    pp, qq, sa, fa, ga, ha, sb, fb, gb, hb,
+    s1l, r1l, s1r, r1r, s2l, r2l, s2r, r2r, sl, rl, sr, rr, sq, rq, s3, r3, s4, r4,
 ):
     rows, cols, width = pair.shape
     nt = cols // ny
@@ -108,7 +110,7 @@
         return (y * 2 + oh, z * 4 + ol * 2 + core)
 
     other_core = (row, z * 4 + xl * 2 + 1 - core)
-    peers = [dev_y(at_y(d)) for d in range(1, ny)] + [dev_z(at_z(d)) for d in range(1, nz)]
+    peers = [dev_y(at_y(d)) for d in far_first(ny)] + [dev_z(at_z(d)) for d in far_first(nz)]
     peers += [dev_x(xh, 1 - xl), dev_x(1 - xh, xl), dev_x(1 - xh, 1 - xl), other_core]
     barrier = pltpu.get_barrier_semaphore()
     for peer in peers:
@@ -129,19 +131,12 @@
     for copy in loads[1:]:
         copy.wait()
 
-    def weight_rows(offset):
-        total = None
-        for side, weight in ((0, w_left), (1, w_right)):
-            r, c, src = one_hot(
-                (2 * chans, 2 * chans), lambda o: (o // (2 * nz)) * nz + o % nz + offset
-            )
-            pick = jnp.where((c == src) & ((r // nz) % 2 == side), 1.0, 0.0).astype(BF16)
-            part = nt_dot(pick, weight[...])
-            total = part if total is None else total + part
-        return total.astype(BF16)
-
-    wt[0:2 * chans, :] = weight_rows(0)
-    wt[2 * chans:4 * chans, :] = weight_rows(chans)
+    _, c, r = one_hot((2 * chans, 2 * chans), lambda o: o)
+    wt[0:2 * chans, :] = nt_dot(jnp.where(c == r, 1.0, 0.0).astype(BF16), w_left[...]).astype(BF16)
+    _, c, r = one_hot(
+        (2 * chans, 2 * chans), lambda o: (o // chans) * chans + (o % ny) * nz + (o % chans) // ny
+    )
+    wt[2 * chans:4 * chans, :] = nt_dot(jnp.where(c == r, 1.0, 0.0).astype(BF16), w_right[...]).astype(BF16)
 
     lane = lax.broadcasted_iota(jnp.int32, (1, lanes), 1)
     row_mask = jnp.zeros((1, lanes), F32)
@@ -164,82 +159,125 @@
         for k in range(ny):
             normed[t, k * rows:(k + 1) * rows, :] = n32[t, pl.ds(k, rows, stride=ny), :].astype(BF16)
         proj = nt_dot(wt[...], normed[t])
-        act = jax.nn.sigmoid(proj[:2 * chans]) * proj[2 * chans:] * mask_of(t)
-        a1[t] = act.astype(BF16).reshape(ny, 2 * nz, lanes)
-
-    def send_y(t):
+        mask = mask_of(t)
+        sides = (proj[:2 * chans], proj[2 * chans:])
+        return [jax.nn.sigmoid(side[:chans]) * side[chans:] * mask for side in sides]
+
+    swap1 = swap_ends(ny, 2, nz)
+    swap2 = swap_ends(ny, 1, nz)
+
+    def send_first(left, left_land, right, right_land, part):
         for d in far_first(ny):
             to = at_y(d)
-            send(a1.at[t, to], b1.at[t, y], s1.at[t], r1.at[t], dev_y(to))
-        b1[t, y] = a1[t, y]
-
-    swap1 = swap_ends(ny, 2, nz)
-
-    def turn(t):
-        take(b1.at[t, pl.ds(0, ny - 1)], r1.at[t])
-        parts = exchange([b1[t, k].astype(F32) for k in range(ny)], rows)
-        stacked = jnp.concatenate(parts, 0).astype(BF16)
-        a2[t] = nn_dot(swap1, stacked).astype(BF16).reshape(nz, 2 * ny, lanes)
+            send(left.at[to], left_land.at[y], s1l.at[part], r1l.at[part], dev_y(to))
         for d in far_first(nz):
             to = at_z(d)
-            send(a2.at[t, to], b2.at[t, z], s2.at[t], r2.at[t], dev_z(to))
-        b2[t, z] = a2[t, z]
-
-    def spread_x(t):
-        take(b2.at[t, pl.ds(0, nz - 1)], r2.at[t])
-        both = b2[t].astype(F32).reshape(nz, 2, ny, lanes)
-        lx[xl, t] = both[:, 0].reshape(nz * ny, lanes).astype(BF16)
-        send(lx.at[xl, t], lx.at[xl, t], sl.at[t], rl.at[t], dev_x(xh, 1 - xl))
-        right = both[:, 1].reshape(nz * ny, lanes).astype(BF16)
-        rs[t] = right
-        send(rs.at[t], rx.at[xl, t], sr.at[t], rr.at[t], dev_x(1 - xh, xh))
+            send(right.at[to], right_land.at[z], s1r.at[part], r1r.at[part], dev_z(to))
+        left_land[y] = left[y]
+        right_land[z] = right[z]
+
+    loads[0].wait()
+    left0, right0 = project(0)
+    left1, right1 = project(1)
+    pairs = lambda u, v, n: jnp.concatenate([u.reshape(n, -1, lanes), v.reshape(n, -1, lanes)], 1).astype(BF16)
+    a1l[...] = pairs(left0, left1, ny)
+    a1r[...] = pairs(right0, right1, nz)
+    pl.semaphore_wait(barrier, len(peers))
+    send_first(a1l, b1l, a1r, b1r, 0)
+    left2, right2 = project(2)
+    for k in range(ny):
+        a1lf[k] = fold(left2[k * nz:(k + 1) * nz]).astype(BF16)
+    for k in range(nz):
+        a1rf[k] = fold(right2[k * ny:(k + 1) * ny]).astype(BF16)
+    send_first(a1lf, b1lf, a1rf, b1rf, 1)
+
+    def turn_right(land, part, out_buf, dst):
+        take(land.at[pl.ds(0, nz - 1)], r1r.at[part])
+        out_buf[...] = nn_dot(swap1, land[...].reshape(nz * 2 * ny, -1)).astype(BF16).reshape(out_buf.shape)
+        for d in far_first(ny):
+            to = at_y(d)
+            send(out_buf.at[to], dst.at[y], s2r.at[part], r2r.at[part, y], dev_y(to))
+        dst[y] = out_buf[y]
+
+    def send_left(out_buf, dst, part):
+        for d in far_first(nz):
+            to = at_z(d)
+            send(out_buf.at[to], dst.at[xl, z], s2l.at[part], r2l.at[part, z], dev_z(to))
+        dst[xl, z] = out_buf[z]
+
+    turn_right(b1r, 0, a2r, b2r)
+    take(b1l.at[pl.ds(0, ny - 1)], r1l.at[0])
+    parts = exchange([b1l[k].astype(F32) for k in range(ny)], rows)
+    a2l[...] = nn_dot(swap1, jnp.concatenate(parts, 0).astype(BF16)).astype(BF16).reshape(a2l.shape)
+    send_left(a2l, b2l, 0)
+    turn_right(b1rf, 1, a2rf, b2rf)
+    take(b1lf.at[pl.ds(0, ny - 1)], r1l.at[1])
+    parts = exchange([unfold(b1lf[k].astype(F32)) for k in range(ny)], rows)
+    turned = nn_dot(swap2, jnp.concatenate(parts, 0).astype(BF16))
+    for k in range(nz):
+        a2lf[k] = fold(turned[k * ny:(k + 1) * ny]).astype(BF16)
+    send_left(a2lf, b2lf, 1)
+
+    for t in range(nt):
+        gate[t] = jax.nn.sigmoid(nn_dot(normed[t], w_gate[...]))
+
+    def forward(left, right, right_dst, part):
+        def forward_left(k):
+            send(left.at[xl, k], left.at[xl, k], sl.at[part], rl.at[part], dev_x(xh, 1 - xl))
+
+        def forward_right(k):
+            send(right.at[k], right_dst.at[xl, k], sr.at[part], rr.at[part], dev_x(1 - xh, xh))
+
+            @pl.when(jnp.logical_not(same))
+            def _():
+                send(right.at[k], right_dst.at[xl, k], sr.at[part], rr.at[part], dev_x(xh, xh))
+
+        forward_right(y)
+        forward_left(z)
+        for d in reversed(far_first(ny)):
+            k = at_y(d)
+            take(right.at[k], r2r.at[part, k])
+            forward_right(k)
+            k = at_z(d)
+            take(left.at[xl, k], r2l.at[part, k])
+            forward_left(k)
 
         @pl.when(same)
         def _():
-            rx[xl, t] = right
+            right_dst[xl] = right[...]
+
+    def gather_x(left, right_dst, part):
+        take(left.at[0], rl.at[part])
+
+        @pl.when(same)
+        def _():
+            take(right_dst.at[0], rr.at[part])
 
         @pl.when(jnp.logical_not(same))
         def _():
-            send(rs.at[t], rx.at[xl, t], sr.at[t], rr.at[t], dev_x(xh, xh))
-
-    def gather_x(t):
-        take(lx.at[0, t], rl.at[t])
-
-        @pl.when(same)
-        def _():
-            take(rx.at[0, t], rr.at[t])
-
-        @pl.when(jnp.logical_not(same))
-        def _():
-            take(rx.at[:, t], rr.at[t])
-
-    loads[0].wait()
-    project(0)
-    pl.semaphore_wait(barrier, len(peers))
-    send_y(0)
-    for t in range(1, nt):
-        project(t)
-        send_y(t)
-    turn(0)
-    turn(1)
-    spread_x(0)
-    turn(2)
-    spread_x(1)
-    for t in range(nt):
-        gate[t] = jax.nn.sigmoid(nn_dot(normed[t], w_gate[...]))
-    spread_x(2)
-
-    half = nz * ny * 2
-    gather_x(0)
-    gather_x(1)
-    first = tn_dot(rx[:, 0:2].reshape(2 * half, lanes), lx[:, 0:2].reshape(2 * half, lanes))
-    gather_x(2)
-    total = first + tn_dot(rx[:, 2].reshape(half, lanes), lx[:, 2].reshape(half, lanes))
+            take(right_dst, rr.at[part])
+
+    forward(b2l, b2r, rx, 0)
+    forward(b2lf, b2rf, rxf, 1)
+
+    two = 2 * ny
+    gather_x(b2l, rx, 0)
+    panels = []
+    for x in range(2):
+        parts = exchange([rx[x, k].astype(F32) for k in range(ny)], rows)
+        panels.append(nn_dot(swap1, jnp.concatenate(parts, 0).astype(BF16)).astype(BF16))
+    total = tn_dot(jnp.concatenate(panels, 0), b2l[...].reshape(2 * nz * two, lanes))
+    gather_x(b2lf, rxf, 1)
+    panels = []
+    for x in range(2):
+        parts = exchange([unfold(rxf[x, k].astype(F32)) for k in range(ny)], rows)
+        panels.append(nn_dot(swap2, jnp.concatenate(parts, 0).astype(BF16)).astype(BF16))
+    lefts = [unfold(b2lf[x, k].astype(F32)) for x in range(2) for k in range(nz)]
+    total = total + tn_dot(jnp.concatenate(panels, 0), jnp.concatenate(lefts, 0).astype(BF16))
     pp[...] = total.reshape(nz, rows, lanes)
     send(pp.at[:, pl.ds((1 - core) * cols, cols), :], qq, sq, rq, other_core)
     take(qq, rq)
     scale = 4.0 / math.sqrt(rows * 2 * ny)
-    two = 2 * ny
 
     tri = (pp[:, pl.ds(core * cols, cols), :] + qq[...]) * scale
     sa[...] = tri[:, :two].astype(BF16)
@@ -286,18 +324,20 @@
     take(hb.at[pl.ds(0, ny - 1)], r4.at[1])
     finish(2, jnp.concatenate([unfold(hb[k].astype(F32)) for k in range(ny)], 0))
 
-    for t in range(nt):
-        take(a1.at[t, pl.ds(0, ny - 1)], s1.at[t])
-        take(a2.at[t, pl.ds(0, nz - 1)], s2.at[t])
-        take(lx.at[0, t], sl.at[t])
+    for part, (first, second, land) in enumerate(((a1l, a2l, rx), (a1lf, a2lf, rxf))):
+        take(first.at[pl.ds(0, ny - 1)], s1l.at[part])
+        take(first.at[pl.ds(0, nz - 1)], s1r.at[part])
+        take(second.at[pl.ds(0, nz - 1)], s2l.at[part])
+        take(second.at[pl.ds(0, ny - 1)], s2r.at[part])
+        take(land.at[0], sl.at[part])
 
         @pl.when(same)
         def _():
-            take(rx.at[0, t], sr.at[t])
+            take(land.at[0], sr.at[part])
 
         @pl.when(jnp.logical_not(same))
         def _():
-            take(rx.at[:, t], sr.at[t])
+            take(land, sr.at[part])
     take(qq, sq)
     take(sa.at[pl.ds(0, nz - 1)], s3.at[0])
     take(sb.at[pl.ds(0, nz - 1)], s3.at[1])
@@ -331,13 +371,24 @@
             pltpu.VMEM((nt, rows * ny, width), BF16),
             pltpu.VMEM((nt, rows * ny, width), F32),
             pltpu.VMEM((4 * chans, width), BF16),
-            pltpu.VMEM((nt, ny, 2 * nz, lanes), BF16),
-            pltpu.VMEM((nt, ny, 2 * nz, lanes), BF16),
-            pltpu.VMEM((nt, nz, 2 * ny, lanes), BF16),
-            pltpu.VMEM((nt, nz, 2 * ny, lanes), BF16),
-            pltpu.VMEM((2, nt, nz * ny, lanes), BF16),
-            pltpu.VMEM((nt, nz * ny, lanes), BF16),
-            pltpu.VMEM((2, nt, nz * ny, lanes), BF16),
+            pltpu.VMEM((ny, 2 * nz, lanes), BF16),
+            pltpu.VMEM((ny, 2 * nz, third), BF16),
+            pltpu.VMEM((ny, 2 * nz, lanes), BF16),
+            pltpu.VMEM((ny, 2 * nz, third), BF16),
+            pltpu.VMEM((nz, 2 * ny, lanes), BF16),
+            pltpu.VMEM((nz, 2 * ny, third), BF16),
+            pltpu.VMEM((nz, 2 * ny, lanes), BF16),
+            pltpu.VMEM((nz, 2 * ny, third), BF16),
+            pltpu.VMEM((nz, 2 * ny, lanes), BF16),
+            pltpu.VMEM((nz, 2 * ny, third), BF16),
+            pltpu.VMEM((2, nz, 2 * ny, lanes), BF16),
+            pltpu.VMEM((2, nz, 2 * ny, third), BF16),
+            pltpu.VMEM((ny, 2 * nz, lanes), BF16),
+            pltpu.VMEM((ny, 2 * nz, third), BF16),
+            pltpu.VMEM((ny, 2 * nz, lanes), BF16),
+            pltpu.VMEM((ny, 2 * nz, third), BF16),
+            pltpu.VMEM((2, ny, 2 * nz, lanes), BF16),
+            pltpu.VMEM((2, ny, 2 * nz, third), BF16),
             pltpu.VMEM((nz, rows, lanes), F32),
             pltpu.VMEM((nz, cols, lanes), F32),
             pltpu.VMEM((nz, 2 * ny, lanes), BF16),
@@ -348,7 +399,7 @@
             pltpu.VMEM((nz, 2 * ny, third), BF16),
             pltpu.VMEM((ny, 2 * nz, third), BF16),
             pltpu.VMEM((ny, 2 * nz, third), BF16),
-        ] + [dma((nt,))] * 8 + [dma, dma] + [dma((2,))] * 4,
+        ] + [dma((2,))] * 4 + [dma((2,)), dma((2, nz)), dma((2,)), dma((2, ny))] + [dma((2,))] * 4 + [dma, dma] + [dma((2,))] * 4,
         compiler_params=pltpu.CompilerParams(
             collective_id=0, has_side_effects=True, vmem_limit_bytes=64 * 1024 * 1024
         ),

time: 50.9 us -> 47.9 us (0.941)
  Pallas kernels: 49 us -> 46 us
    pallas_call x1, Pallas kernels: 49 us -> 46 us  [per_device(): pl.pallas_call(functools.partial(kernel, ny, nz), out_shape=jax.ShapeDtyp...]
where the time goes in v3:
time: 47.9 us; the launch traced here: 47.8 us
  Pallas kernels  46 us (96%)
  local copies, waits for them, and re-layouts  1.75 us (4%)
    pallas_call x1, Pallas kernels, per_device(): pl.pallas_call(functools.partial(kernel, ny, nz), out_shape=jax.ShapeDtyp...  46 us
    transpose x1, local copies, waits for them, and re-layouts, per_device(): return jnp.transpose(swapped, (1, 0, 2))  1.75 us

profile of v3, /device:TPU:1, one launch (start us, length us, event | category | flops | bytes accessed | tf_op | source)
XLA Modules:
  0.0 47.8 jit_solution(14818897006872605950)
XLA Ops:
  0.0 46.0 %shard_map.82 = bf16[24,48,128]{2,1,0:T(8,128)(2,1)} custom-call(s32[768]{0:T(1024)} %tm_hbm.1, bf16[48,24,128]{2,1,0:T(8,128)(2,1)} %pair_hbm.1, f32[1,128]{1,0:T(1,128)} %bitcast.4, f32[1,128]{1,0:T(1,128)} %bitcast.5, bf16[128,128]{1,0:T(8,128)(2,1)} %wl_hbm.1, bf16[128,128]{1,0:T(8,128)(2,1)} %wr_hbm.1, bf16[128,128]{1,0:T(8,128)(2,1)} %wg_hbm.1, ...), custom_call_target="tpu_custom_call" | custom-call | tf_op jit(solution)/shard_map/pallas_call | solution.py:355
  46.0 1.8 %copy.9 = bf16[48,24,128]{2,1,0:T(8,128)(2,1)} copy(bf16[48,24,128]{2,0,1:T(8,128)(2,1)} %bitcast.3) | data formatting | bytes 589824 | tf_op jit(solution)/shard_map/transpose | solution.py:407

commit v4 on v3

--- a/solution.py
+++ b/solution.py
@@ -205,18 +205,18 @@
             send(out_buf.at[to], dst.at[xl, z], s2l.at[part], r2l.at[part, z], dev_z(to))
         dst[xl, z] = out_buf[z]
 
-    turn_right(b1r, 0, a2r, b2r)
     take(b1l.at[pl.ds(0, ny - 1)], r1l.at[0])
     parts = exchange([b1l[k].astype(F32) for k in range(ny)], rows)
     a2l[...] = nn_dot(swap1, jnp.concatenate(parts, 0).astype(BF16)).astype(BF16).reshape(a2l.shape)
     send_left(a2l, b2l, 0)
-    turn_right(b1rf, 1, a2rf, b2rf)
+    turn_right(b1r, 0, a2r, b2r)
     take(b1lf.at[pl.ds(0, ny - 1)], r1l.at[1])
     parts = exchange([unfold(b1lf[k].astype(F32)) for k in range(ny)], rows)
     turned = nn_dot(swap2, jnp.concatenate(parts, 0).astype(BF16))
     for k in range(nz):
         a2lf[k] = fold(turned[k * ny:(k + 1) * ny]).astype(BF16)
     send_left(a2lf, b2lf, 1)
+    turn_right(b1rf, 1, a2rf, b2rf)
 
     for t in range(nt):
         gate[t] = jax.nn.sigmoid(nn_dot(normed[t], w_gate[...]))
@@ -273,22 +273,29 @@
         parts = exchange([unfold(rxf[x, k].astype(F32)) for k in range(ny)], rows)
         panels.append(nn_dot(swap2, jnp.concatenate(parts, 0).astype(BF16)).astype(BF16))
     lefts = [unfold(b2lf[x, k].astype(F32)) for x in range(2) for k in range(nz)]
-    total = total + tn_dot(jnp.concatenate(panels, 0), jnp.concatenate(lefts, 0).astype(BF16))
-    pp[...] = total.reshape(nz, rows, lanes)
-    send(pp.at[:, pl.ds((1 - core) * cols, cols), :], qq, sq, rq, other_core)
-    take(qq, rq)
+    right, left = jnp.concatenate(panels, 0), jnp.concatenate(lefts, 0).astype(BF16)
     scale = 4.0 / math.sqrt(rows * 2 * ny)
-
-    tri = (pp[:, pl.ds(core * cols, cols), :] + qq[...]) * scale
-    sa[...] = tri[:, :two].astype(BF16)
-    for d in far_first(nz):
-        to = at_z(d)
-        send(sa.at[to], fa.at[z], s3.at[0], r3.at[0], dev_z(to))
-    for k in range(nz):
-        sb[k] = fold(tri[k, two:]).astype(BF16)
-    for d in far_first(nz):
-        to = at_z(d)
-        send(sb.at[to], fb.at[z], s3.at[1], r3.at[1], dev_z(to))
+    cut = lanes // 3
+    ahead = max(1, cut // rows)
+    groups = ((0, ahead, -(-ahead * rows // cut) * cut), (ahead, nz, lanes))
+
+    done = 0
+    for g, (low, high, until) in enumerate(groups):
+        pp[done:until] = total[done:until] + tn_dot(right[:, done:until], left)
+        done = until
+        for k in range(low, high):
+            send(pp.at[pl.ds(k * rows + (1 - core) * cols, cols)], qq.at[k], sq.at[g], rq.at[g], other_core)
+    for g, (low, high, _) in enumerate(groups):
+        take(qq.at[pl.ds(low, high - low)], rq.at[g])
+        for k in range(low, high):
+            tri = (pp[pl.ds(k * rows + core * cols, cols), :] + qq[k]) * scale
+            sa[k] = tri[:two].astype(BF16)
+            sb[k] = fold(tri[two:]).astype(BF16)
+
+            @pl.when(z != k)
+            def _():
+                send(sa.at[k], fa.at[z], s3.at[0], r3.at[0], dev_z(k))
+                send(sb.at[k], fb.at[z], s3.at[1], r3.at[1], dev_z(k))
     fa[z] = sa[z]
     fb[z] = sb[z]
 
@@ -338,7 +345,8 @@
         @pl.when(jnp.logical_not(same))
         def _():
             take(land, sr.at[part])
-    take(qq, sq)
+    for g, (low, high, _) in enumerate(groups):
+        take(qq.at[pl.ds(low, high - low)], sq.at[g])
     take(sa.at[pl.ds(0, nz - 1)], s3.at[0])
     take(sb.at[pl.ds(0, nz - 1)], s3.at[1])
     take(ga.at[pl.ds(0, ny - 1)], s4.at[0])
@@ -354,7 +362,7 @@
     dma = pltpu.SemaphoreType.DMA
     swapped = pl.pallas_call(
         functools.partial(kernel, ny, nz),
-        out_shape=jax.ShapeDtypeStruct((cols, rows, width), BF16),
+        out_shape=pltpu.VMEM((cols, rows, width), BF16),
         in_specs=[pl.BlockSpec(memory_space=pl.ANY)] * 8,
         out_specs=pl.BlockSpec(memory_space=pltpu.VMEM),
         scratch_shapes=[
@@ -389,7 +397,7 @@
             pltpu.VMEM((ny, 2 * nz, third), BF16),
             pltpu.VMEM((2, ny, 2 * nz, lanes), BF16),
             pltpu.VMEM((2, ny, 2 * nz, third), BF16),
-            pltpu.VMEM((nz, rows, lanes), F32),
+            pltpu.VMEM((lanes, lanes), F32),
             pltpu.VMEM((nz, cols, lanes), F32),
             pltpu.VMEM((nz, 2 * ny, lanes), BF16),
             pltpu.VMEM((nz, 2 * ny, lanes), BF16),
@@ -399,9 +407,9 @@
             pltpu.VMEM((nz, 2 * ny, third), BF16),
             pltpu.VMEM((ny, 2 * nz, third), BF16),
             pltpu.VMEM((ny, 2 * nz, third), BF16),
-        ] + [dma((2,))] * 4 + [dma((2,)), dma((2, nz)), dma((2,)), dma((2, ny))] + [dma((2,))] * 4 + [dma, dma] + [dma((2,))] * 4,
+        ] + [dma((2,))] * 4 + [dma((2,)), dma((2, nz)), dma((2,)), dma((2, ny))] + [dma((2,))] * 10,
         compiler_params=pltpu.CompilerParams(
-            collective_id=0, has_side_effects=True, vmem_limit_bytes=64 * 1024 * 1024
+            collective_id=0, has_side_effects=True, vmem_limit_bytes=60 * 1024 * 1024
         ),
     )(token_mask, pair, ln_gain.reshape(1, width), ln_bias.reshape(1, width), w_left, w_right, w_gate, w_out)
     return jnp.transpose(swapped, (1, 0, 2))

time: 47.9 us -> 45.2 us (0.944)
  Pallas kernels: 46 us -> 44 us
  local copies, waits for them, and re-layouts: 1.75 us -> 0.79 us
    pallas_call x1, Pallas kernels: 46 us -> 44 us  [per_device(): pl.pallas_call(functools.partial(kernel, ny, nz), out_shape=pltpu.VMEM((c...]
    transpose x1, local copies, waits for them, and re-layouts: 1.75 us -> 0.79 us  [per_device(): return jnp.transpose(swapped, (1, 0, 2))]
where the time goes in v4:
time: 45.2 us; the launch traced here: 44.8 us
  Pallas kernels  44 us (97%)
  local copies, waits for them, and re-layouts  0.79 us (2%)
    pallas_call x1, Pallas kernels, per_device(): pl.pallas_call(functools.partial(kernel, ny, nz), out_shape=pltpu.VMEM((c...  44 us

profile of v4, /device:TPU:1, one launch (start us, length us, event | category | flops | bytes accessed | tf_op | source)
XLA Modules:
  0.0 44.8 jit_solution(5867359746182998313)
XLA Ops:
  0.0 44.0 %shard_map.82 = bf16[24,48,128]{2,1,0:T(8,128)(2,1)S(1)} custom-call(s32[768]{0:T(1024)} %tm_hbm.1, bf16[48,24,128]{2,1,0:T(8,128)(2,1)} %pair_hbm.1, f32[1,128]{1,0:T(1,128)} %bitcast.4, f32[1,128]{1,0:T(1,128)} %bitcast.5, bf16[128,128]{1,0:T(8,128)(2,1)} %wl_hbm.1, bf16[128,128]{1,0:T(8,128)(2,1)} %wr_hbm.1, bf16[128,128]{1,0:T(8,128)(2,1)} %wg_hbm.1, ...), custom_call_target="tpu_custom_call" | custom-call | tf_op jit(solution)/shard_map/pallas_call | solution.py:363
  44.0 0.8 %copy.9 = bf16[48,24,128]{2,1,0:T(8,128)(2,1)} copy(bf16[48,24,128]{2,0,1:T(8,128)(2,1)S(1)} %bitcast.3) | data formatting | bytes 589824 | tf_op jit(solution)/shard_map/transpose | solution.py:415

commit v5 on v4

--- a/solution.py
+++ b/solution.py
@@ -44,18 +44,23 @@
     return lax.dot_general(x, y, (((1,), (0,)), ((), ())), preferred_element_type=F32)
 
 
-def exchange(parts, width):
-    n = len(parts)
-    total = n * width
-    pos = lax.broadcasted_iota(jnp.int32, parts[0].shape, 1) // width
-    rolled = [parts[0]] + [pltpu.roll(parts[y], y * width, 1) for y in range(1, n)]
-    result = []
-    for k in range(n):
-        picked = rolled[0]
-        for y in range(1, n):
-            picked = jnp.where(pos == (k + y) % n, rolled[y], picked)
-        result.append(picked if k == 0 else pltpu.roll(picked, total - k * width, 1))
-    return result
+def spread(parts, width):
+    return [pltpu.roll(part, y * width, 1) if y else part for y, part in enumerate(parts)]
+
+
+def pick(rolled, width, k, keep=None):
+    total = rolled[0].shape[1]
+    n = total // width
+    pos = lax.broadcasted_iota(jnp.int32, rolled[0].shape, 1) // width
+    picked = rolled[0]
+    for y, part in list(enumerate(rolled))[1:]:
+        picked = jnp.where(pos == (k + y) % n, part, picked)
+    return (pltpu.roll(picked, total - k * width, 1) if k else picked)[:, :keep]
+
+
+def exchange(parts, width, keep=None):
+    rolled = spread(parts, width)
+    return [pick(rolled, width, k, keep) for k in range(parts[0].shape[1] // width)]
 
 
 def fold(block):
@@ -221,71 +226,84 @@
     for t in range(nt):
         gate[t] = jax.nn.sigmoid(nn_dot(normed[t], w_gate[...]))
 
-    def forward(left, right, right_dst, part):
-        def forward_left(k):
-            send(left.at[xl, k], left.at[xl, k], sl.at[part], rl.at[part], dev_x(xh, 1 - xl))
-
-        def forward_right(k):
-            send(right.at[k], right_dst.at[xl, k], sr.at[part], rr.at[part], dev_x(1 - xh, xh))
+    ahead = max(1, lanes // (3 * rows))
+    cut = -(-ahead * rows * 3 // lanes) * (lanes // 3)
+    groups = ((0, ahead), (ahead, nz))
+
+    def forward_left(left, part, k):
+        send(left.at[xl, k], left.at[xl, k], sl.at[part], rl.at[part], dev_x(xh, 1 - xl))
+
+    def forward_right(right, dst, part, g):
+        low, high = groups[g]
+        for k in range(low, high):
+            @pl.when(y != k)
+            def _():
+                take(right.at[k], r2r.at[part, k])
+
+            send(right.at[k], dst.at[xl, k], sr.at[part, g], rr.at[part, g], dev_x(1 - xh, xh))
 
             @pl.when(jnp.logical_not(same))
             def _():
-                send(right.at[k], right_dst.at[xl, k], sr.at[part], rr.at[part], dev_x(xh, xh))
-
-        forward_right(y)
-        forward_left(z)
-        for d in reversed(far_first(ny)):
-            k = at_y(d)
-            take(right.at[k], r2r.at[part, k])
-            forward_right(k)
+                send(right.at[k], dst.at[xl, k], sr.at[part, g], rr.at[part, g], dev_x(xh, xh))
+
+        @pl.when(same)
+        def _():
+            dst[xl, low:high] = right[low:high]
+
+    for part, (left, right, dst) in enumerate(((b2l, b2r, rx), (b2lf, b2rf, rxf))):
+        forward_left(left, part, z)
+        order = far_first(nz)[::-1]
+        for place, d in enumerate(order):
+            if place == len(order) // 2:
+                forward_right(right, dst, part, 0)
             k = at_z(d)
             take(left.at[xl, k], r2l.at[part, k])
-            forward_left(k)
+            forward_left(left, part, k)
+    forward_right(b2r, rx, 0, 1)
+    forward_right(b2rf, rxf, 1, 1)
+
+    two = 2 * ny
+
+    def take_right(dst, part, g, sem):
+        low, high = groups[g]
 
         @pl.when(same)
         def _():
-            right_dst[xl] = right[...]
-
-    def gather_x(left, right_dst, part):
-        take(left.at[0], rl.at[part])
-
-        @pl.when(same)
-        def _():
-            take(right_dst.at[0], rr.at[part])
+            take(dst.at[0, pl.ds(low, high - low)], sem.at[part, g])
 
         @pl.when(jnp.logical_not(same))
         def _():
-            take(right_dst, rr.at[part])
-
-    forward(b2l, b2r, rx, 0)
-    forward(b2lf, b2rf, rxf, 1)
-
-    two = 2 * ny
-    gather_x(b2l, rx, 0)
-    panels = []
-    for x in range(2):
-        parts = exchange([rx[x, k].astype(F32) for k in range(ny)], rows)
-        panels.append(nn_dot(swap1, jnp.concatenate(parts, 0).astype(BF16)).astype(BF16))
-    total = tn_dot(jnp.concatenate(panels, 0), b2l[...].reshape(2 * nz * two, lanes))
-    gather_x(b2lf, rxf, 1)
-    panels = []
-    for x in range(2):
-        parts = exchange([unfold(rxf[x, k].astype(F32)) for k in range(ny)], rows)
-        panels.append(nn_dot(swap2, jnp.concatenate(parts, 0).astype(BF16)).astype(BF16))
-    lefts = [unfold(b2lf[x, k].astype(F32)) for x in range(2) for k in range(nz)]
-    right, left = jnp.concatenate(panels, 0), jnp.concatenate(lefts, 0).astype(BF16)
+            take(dst.at[:, pl.ds(low, high - low)], sem.at[part, g])
+
+    def panel(g):
+        count, keep = (ahead, cut) if g == 0 else (ny, lanes)
+
+        def stack(parts, swap):
+            return nn_dot(swap, jnp.concatenate(exchange(parts, rows, keep), 0).astype(BF16)).astype(BF16)
+
+        return (
+            lambda: jnp.concatenate([stack([rx[x, k].astype(F32) for k in range(count)], swap1) for x in range(2)], 0),
+            lambda: jnp.concatenate(
+                [stack([unfold(rxf[x, k].astype(F32)) for k in range(count)], swap2) for x in range(2)], 0
+            ),
+        )
+
     scale = 4.0 / math.sqrt(rows * 2 * ny)
-    cut = lanes // 3
-    ahead = max(1, cut // rows)
-    groups = ((0, ahead, -(-ahead * rows // cut) * cut), (ahead, nz, lanes))
-
-    done = 0
-    for g, (low, high, until) in enumerate(groups):
-        pp[done:until] = total[done:until] + tn_dot(right[:, done:until], left)
-        done = until
+    for g, (low, high) in enumerate(groups):
+        if g == 0:
+            take(b2l.at[0], rl.at[0])
+        take_right(rx, 0, g, rr)
+        panel_a, panel_b = panel(g)
+        total = tn_dot(panel_a(), b2l[...].reshape(2 * nz * two, lanes))
+        if g == 0:
+            take(b2lf.at[0], rl.at[1])
+            lefts = [unfold(b2lf[x, k].astype(F32)) for x in range(2) for k in range(nz)]
+            left_b = jnp.concatenate(lefts, 0).astype(BF16)
+        take_right(rxf, 1, g, rr)
+        total = total + tn_dot(panel_b(), left_b)
+        pp[low * rows:high * rows] = total[low * rows:high * rows]
         for k in range(low, high):
             send(pp.at[pl.ds(k * rows + (1 - core) * cols, cols)], qq.at[k], sq.at[g], rq.at[g], other_core)
-    for g, (low, high, _) in enumerate(groups):
         take(qq.at[pl.ds(low, high - low)], rq.at[g])
         for k in range(low, high):
             tri = (pp[pl.ds(k * rows + core * cols, cols), :] + qq[k]) * scale
@@ -301,23 +319,20 @@
 
     take(fa.at[pl.ds(0, nz - 1)], r3.at[0])
     turned = nn_dot(swap_ends(nz, 2, ny), fa[...].reshape(nz * two, lanes)).reshape(ny, 2 * nz, lanes)
-    parts = exchange([turned[j] for j in range(ny)], rows)
-    for k in range(ny):
-        ga[k] = parts[k].astype(BF16)
-    for d in far_first(ny):
-        to = at_y(d)
-        send(ga.at[to], ha.at[y], s4.at[0], r4.at[0], dev_y(to))
-    ha[y] = ga[y]
-
+    rolled_a = spread([turned[j] for j in range(ny)], rows)
     take(fb.at[pl.ds(0, nz - 1)], r3.at[1])
     flat = jnp.concatenate([unfold(fb[k].astype(F32)) for k in range(nz)], 0).astype(BF16)
     turned = nn_dot(swap_ends(nz, 1, ny), flat).reshape(ny, nz, lanes)
-    parts = exchange([turned[j] for j in range(ny)], rows)
-    for k in range(ny):
-        gb[k] = fold(parts[k]).astype(BF16)
-    for d in far_first(ny):
-        to = at_y(d)
-        send(gb.at[to], hb.at[y], s4.at[1], r4.at[1], dev_y(to))
+    rolled_b = spread([turned[j] for j in range(ny)], rows)
+    for k in sorted(range(ny), key=lambda k: min(k, ny - k + 1.6)):
+        ga[k] = pick(rolled_a, rows, k).astype(BF16)
+        gb[k] = fold(pick(rolled_b, rows, k)).astype(BF16)
+
+        @pl.when(y != k)
+        def _():
+            send(ga.at[k], ha.at[y], s4.at[0], r4.at[0], dev_y(k))
+            send(gb.at[k], hb.at[y], s4.at[1], r4.at[1], dev_y(k))
+    ha[y] = ga[y]
     hb[y] = gb[y]
 
     def finish(t, block):
@@ -338,14 +353,9 @@
         take(second.at[pl.ds(0, ny - 1)], s2r.at[part])
         take(land.at[0], sl.at[part])
 
-        @pl.when(same)
-        def _():
-            take(land.at[0], sr.at[part])
-
-        @pl.when(jnp.logical_not(same))
-        def _():
-            take(land, sr.at[part])
-    for g, (low, high, _) in enumerate(groups):
+        for g in range(2):
+            take_right(land, part, g, sr)
+    for g, (low, high) in enumerate(groups):
         take(qq.at[pl.ds(low, high - low)], sq.at[g])
     take(sa.at[pl.ds(0, nz - 1)], s3.at[0])
     take(sb.at[pl.ds(0, nz - 1)], s3.at[1])
@@ -407,7 +417,7 @@
             pltpu.VMEM((nz, 2 * ny, third), BF16),
             pltpu.VMEM((ny, 2 * nz, third), BF16),
             pltpu.VMEM((ny, 2 * nz, third), BF16),
-        ] + [dma((2,))] * 4 + [dma((2,)), dma((2, nz)), dma((2,)), dma((2, ny))] + [dma((2,))] * 10,
+        ] + [dma((2,))] * 4 + [dma((2,)), dma((2, nz)), dma((2,)), dma((2, ny))] + [dma((2,))] * 2 + [dma((2, 2))] * 2 + [dma((2,))] * 6,
         compiler_params=pltpu.CompilerParams(
             collective_id=0, has_side_effects=True, vmem_limit_bytes=60 * 1024 * 1024
         ),

time: 45.2 us -> 43.8 us (0.969)
  the two profiles are of different devices: /device:TPU:1 before, /device:TPU:2 now
where the time goes in v5:
time: 43.8 us; the launch traced here: 43.6 us
  Pallas kernels  42.8 us (98%)
  local copies, waits for them, and re-layouts  0.79 us (2%)
    pallas_call x1, Pallas kernels, per_device(): pl.pallas_call(functools.partial(kernel, ny, nz), out_shape=pltpu.VMEM((c...  42.8 us

profile of v5, /device:TPU:2, one launch (start us, length us, event | category | flops | bytes accessed | tf_op | source)
XLA Modules:
  0.0 43.6 jit_solution(2726419153718899387)
XLA Ops:
  0.0 42.8 %shard_map.82 = bf16[24,48,128]{2,1,0:T(8,128)(2,1)S(1)} custom-call(s32[768]{0:T(1024)} %tm_hbm.1, bf16[48,24,128]{2,1,0:T(8,128)(2,1)} %pair_hbm.1, f32[1,128]{1,0:T(1,128)} %bitcast.4, f32[1,128]{1,0:T(1,128)} %bitcast.5, bf16[128,128]{1,0:T(8,128)(2,1)} %wl_hbm.1, bf16[128,128]{1,0:T(8,128)(2,1)} %wr_hbm.1, bf16[128,128]{1,0:T(8,128)(2,1)} %wg_hbm.1, ...), custom_call_target="tpu_custom_call" | custom-call | tf_op jit(solution)/shard_map/pallas_call | solution.py:373
  42.8 0.8 %copy.9 = bf16[48,24,128]{2,1,0:T(8,128)(2,1)} copy(bf16[48,24,128]{2,0,1:T(8,128)(2,1)S(1)} %bitcast.3) | data formatting | bytes 589824 | tf_op jit(solution)/shard_map/transpose | solution.py:425

commit v6 on v5

--- a/solution.py
+++ b/solution.py
@@ -80,8 +80,8 @@
     ny, nz, tm_hbm, pair_hbm, gain_hbm, bias_hbm, wl_hbm, wr_hbm, wg_hbm, wo_hbm, out,
     tm, pair, gain, bias, w_left, w_right, w_gate, w_out, load, n32, normed, gate, wt,
     a1l, a1lf, b1l, b1lf, a1r, a1rf, b1r, b1rf, a2l, a2lf, b2l, b2lf, a2r, a2rf, b2r, b2rf, rx, rxf,
-    pp, qq, sa, fa, ga, ha, sb, fb, gb, hb,
-    s1l, r1l, s1r, r1r, s2l, r2l, s2r, r2r, sl, rl, sr, rr, sq, rq, s3, r3, s4, r4,
+    pp, qq, sc, land, f32,
+    s1l, r1l, s1r, r1r, s2l, r2l, s2r, r2r, sl, rl, sr, rr, sq, rq, s3, r3,
 ):
     rows, cols, width = pair.shape
     nt = cols // ny
@@ -289,6 +289,21 @@
         )
 
     scale = 4.0 / math.sqrt(rows * 2 * ny)
+    mine = y * nz + z
+    tile_lanes = land.shape[2]
+
+    def tile(tri, o):
+        base, off = divmod(o * rows, tile_lanes)
+        lane = lax.broadcasted_iota(jnp.int32, (cols, tile_lanes), 1)
+        block = tri[:, base * tile_lanes:(base + 1) * tile_lanes]
+        if off:
+            block = pltpu.roll(block, tile_lanes - off, 1)
+        if off + rows > tile_lanes:
+            after = pltpu.roll(tri[:, (base + 1) * tile_lanes:(base + 2) * tile_lanes], tile_lanes - off, 1)
+            block = jnp.where(lane < tile_lanes - off, block, after)
+        top = jnp.where(lane[:ny] < rows, block[:ny], pltpu.roll(block[ny:two], rows, 1))
+        return jnp.concatenate([top, block[two:]], 0)
+
     for g, (low, high) in enumerate(groups):
         if g == 0:
             take(b2l.at[0], rl.at[0])
@@ -307,60 +322,43 @@
         take(qq.at[pl.ds(low, high - low)], rq.at[g])
         for k in range(low, high):
             tri = (pp[pl.ds(k * rows + core * cols, cols), :] + qq[k]) * scale
-            sa[k] = tri[:two].astype(BF16)
-            sb[k] = fold(tri[two:]).astype(BF16)
+            for o in range(ny):
+                sc[k, o] = tile(tri, o).astype(BF16)
+            for d in far_first(ny):
+                to = at_y(d)
+                send(sc.at[k, to], land.at[mine], s3, r3, (to * 2 + xh, k * 4 + xl * 2 + core))
 
             @pl.when(z != k)
             def _():
-                send(sa.at[k], fa.at[z], s3.at[0], r3.at[0], dev_z(k))
-                send(sb.at[k], fb.at[z], s3.at[1], r3.at[1], dev_z(k))
-    fa[z] = sa[z]
-    fb[z] = sb[z]
-
-    take(fa.at[pl.ds(0, nz - 1)], r3.at[0])
-    turned = nn_dot(swap_ends(nz, 2, ny), fa[...].reshape(nz * two, lanes)).reshape(ny, 2 * nz, lanes)
-    rolled_a = spread([turned[j] for j in range(ny)], rows)
-    take(fb.at[pl.ds(0, nz - 1)], r3.at[1])
-    flat = jnp.concatenate([unfold(fb[k].astype(F32)) for k in range(nz)], 0).astype(BF16)
-    turned = nn_dot(swap_ends(nz, 1, ny), flat).reshape(ny, nz, lanes)
-    rolled_b = spread([turned[j] for j in range(ny)], rows)
-    for k in sorted(range(ny), key=lambda k: min(k, ny - k + 1.6)):
-        ga[k] = pick(rolled_a, rows, k).astype(BF16)
-        gb[k] = fold(pick(rolled_b, rows, k)).astype(BF16)
-
-        @pl.when(y != k)
-        def _():
-            send(ga.at[k], ha.at[y], s4.at[0], r4.at[0], dev_y(k))
-            send(gb.at[k], hb.at[y], s4.at[1], r4.at[1], dev_y(k))
-    ha[y] = ga[y]
-    hb[y] = gb[y]
-
-    def finish(t, block):
-        mixed = tn_dot(block.reshape(chans, lanes).astype(BF16), w_out[...])
-        out[t * ny:(t + 1) * ny] = (gate[t] * mixed).astype(BF16).reshape(ny, rows, width)
-
-    take(ha.at[pl.ds(0, ny - 1)], r4.at[0])
-    both = ha[...].astype(F32).reshape(ny, 2, nz, lanes)
-    finish(0, both[:, 0])
-    finish(1, both[:, 1])
-    take(hb.at[pl.ds(0, ny - 1)], r4.at[1])
-    finish(2, jnp.concatenate([unfold(hb[k].astype(F32)) for k in range(ny)], 0))
-
-    for part, (first, second, land) in enumerate(((a1l, a2l, rx), (a1lf, a2lf, rxf))):
+                send(sc.at[k, y], land.at[mine], s3, r3, dev_z(k))
+    land[mine] = sc[z, y]
+
+    take(land.at[pl.ds(0, chans - 1)], r3)
+    f32[...] = land[...].astype(F32).reshape(f32.shape)
+    picked = [f32[pl.ds(r, chans, stride=two), :] for r in range(two)]
+    side = lax.broadcasted_iota(jnp.int32, picked[0].shape, 1) < rows
+    for r in range(ny, two, 2):
+        picked[r] = jnp.where(side, picked[r], pltpu.roll(picked[r + 1], rows, 1))
+    places = [(r, r + ny) for r in range(ny)] + [(r, r + 1) for r in range(two, cols, 2)]
+    mixed = tn_dot(jnp.concatenate(picked[:ny] + picked[ny::2], 1).astype(BF16), w_out[...])
+    for index, pair_of in enumerate(places):
+        for half, j in enumerate(pair_of):
+            start = index * tile_lanes + half * rows
+            t, at = j // ny, j % ny * rows
+            out[j] = (gate[t, at:at + rows, :] * mixed[start:start + rows]).astype(BF16)
+
+    for part, (first, second, third) in enumerate(((a1l, a2l, rx), (a1lf, a2lf, rxf))):
         take(first.at[pl.ds(0, ny - 1)], s1l.at[part])
         take(first.at[pl.ds(0, nz - 1)], s1r.at[part])
         take(second.at[pl.ds(0, nz - 1)], s2l.at[part])
         take(second.at[pl.ds(0, ny - 1)], s2r.at[part])
-        take(land.at[0], sl.at[part])
+        take(third.at[0], sl.at[part])
 
         for g in range(2):
-            take_right(land, part, g, sr)
+            take_right(third, part, g, sr)
     for g, (low, high) in enumerate(groups):
         take(qq.at[pl.ds(low, high - low)], sq.at[g])
-    take(sa.at[pl.ds(0, nz - 1)], s3.at[0])
-    take(sb.at[pl.ds(0, nz - 1)], s3.at[1])
-    take(ga.at[pl.ds(0, ny - 1)], s4.at[0])
-    take(gb.at[pl.ds(0, ny - 1)], s4.at[1])
+    take(land.at[pl.ds(0, chans - 1)], s3)
 
 
 def per_device(ny, nz, pair, token_mask, ln_gain, ln_bias, w_left, w_right, w_gate, w_out):
@@ -409,15 +407,10 @@
             pltpu.VMEM((2, ny, 2 * nz, third), BF16),
             pltpu.VMEM((lanes, lanes), F32),
             pltpu.VMEM((nz, cols, lanes), F32),
-            pltpu.VMEM((nz, 2 * ny, lanes), BF16),
-            pltpu.VMEM((nz, 2 * ny, lanes), BF16),
-            pltpu.VMEM((ny, 2 * nz, lanes), BF16),
-            pltpu.VMEM((ny, 2 * nz, lanes), BF16),
-            pltpu.VMEM((nz, 2 * ny, third), BF16),
-            pltpu.VMEM((nz, 2 * ny, third), BF16),
-            pltpu.VMEM((ny, 2 * nz, third), BF16),
-            pltpu.VMEM((ny, 2 * nz, third), BF16),
-        ] + [dma((2,))] * 4 + [dma((2,)), dma((2, nz)), dma((2,)), dma((2, ny))] + [dma((2,))] * 2 + [dma((2, 2))] * 2 + [dma((2,))] * 6,
+            pltpu.VMEM((nz, ny, 2 * ny, min(lanes, 128)), BF16),
+            pltpu.VMEM((chans, 2 * ny, min(lanes, 128)), BF16),
+            pltpu.VMEM((chans * 2 * ny, min(lanes, 128)), F32),
+        ] + [dma((2,))] * 4 + [dma((2,)), dma((2, nz)), dma((2,)), dma((2, ny))] + [dma((2,))] * 2 + [dma((2, 2))] * 2 + [dma((2,))] * 2 + [dma] * 2,
         compiler_params=pltpu.CompilerParams(
             collective_id=0, has_side_effects=True, vmem_limit_bytes=60 * 1024 * 1024
         ),

time: 43.8 us -> 40.9 us (0.934)
  the two profiles are of different devices: /device:TPU:2 before, /device:TPU:1 now
where the time goes in v6:
time: 40.9 us; the launch traced here: 40.5 us
  Pallas kernels  39.7 us (97%)
  local copies, waits for them, and re-layouts  0.79 us (2%)
    pallas_call x1, Pallas kernels, per_device(): pl.pallas_call(functools.partial(kernel, ny, nz), out_shape=pltpu.VMEM((c...  39.7 us

profile of v6, /device:TPU:1, one launch (start us, length us, event | category | flops | bytes accessed | tf_op | source)
XLA Modules:
  0.0 40.5 jit_solution(9398285697081822259)
XLA Ops:
  0.0 39.7 %shard_map.82 = bf16[24,48,128]{2,1,0:T(8,128)(2,1)S(1)} custom-call(s32[768]{0:T(1024)} %tm_hbm.1, bf16[48,24,128]{2,1,0:T(8,128)(2,1)} %pair_hbm.1, f32[1,128]{1,0:T(1,128)} %bitcast.4, f32[1,128]{1,0:T(1,128)} %bitcast.5, bf16[128,128]{1,0:T(8,128)(2,1)} %wl_hbm.1, bf16[128,128]{1,0:T(8,128)(2,1)} %wr_hbm.1, bf16[128,128]{1,0:T(8,128)(2,1)} %wg_hbm.1, ...), custom_call_target="tpu_custom_call" | custom-call | tf_op jit(solution)/shard_map/pallas_call | solution.py:371
  39.7 0.8 %copy.9 = bf16[48,24,128]{2,1,0:T(8,128)(2,1)} copy(bf16[48,24,128]{2,0,1:T(8,128)(2,1)S(1)} %bitcast.3) | data formatting | bytes 589824 | tf_op jit(solution)/shard_map/transpose | solution.py:418

commit v7 on v6

--- a/solution.py
+++ b/solution.py
@@ -83,7 +83,7 @@
     pp, qq, sc, land, f32,
     s1l, r1l, s1r, r1r, s2l, r2l, s2r, r2r, sl, rl, sr, rr, sq, rq, s3, r3,
 ):
-    rows, cols, width = pair.shape
+    cols, rows, width = out.shape
     nt = cols // ny
     lanes = ny * rows
     chans = ny * nz
@@ -155,7 +155,7 @@
         return row_mask * col_mask
 
     def project(t):
-        block = pair[:, t * ny:(t + 1) * ny, :].astype(F32)
+        block = pair[...].astype(F32).reshape(rows, cols, width)[:, t * ny:(t + 1) * ny, :]
         center = jnp.mean(block, axis=-1, keepdims=True)
         delta = block - center
         spread = jnp.mean(delta * delta, axis=-1, keepdims=True)
@@ -278,13 +278,13 @@
     def panel(g):
         count, keep = (ahead, cut) if g == 0 else (ny, lanes)
 
-        def stack(parts, swap):
-            return nn_dot(swap, jnp.concatenate(exchange(parts, rows, keep), 0).astype(BF16)).astype(BF16)
+        def stack(parts):
+            return jnp.concatenate(exchange(parts, rows, keep), 0).astype(BF16)
 
         return (
-            lambda: jnp.concatenate([stack([rx[x, k].astype(F32) for k in range(count)], swap1) for x in range(2)], 0),
+            lambda: jnp.concatenate([stack([rx[x, k].astype(F32) for k in range(count)]) for x in range(2)], 0),
             lambda: jnp.concatenate(
-                [stack([unfold(rxf[x, k].astype(F32)) for k in range(count)], swap2) for x in range(2)], 0
+                [stack([unfold(rxf[x, k].astype(F32)) for k in range(count)]) for x in range(2)], 0
             ),
         )
 
@@ -307,13 +307,15 @@
     for g, (low, high) in enumerate(groups):
         if g == 0:
             take(b2l.at[0], rl.at[0])
+            left_a = [nn_dot(swap1, b2l[x].reshape(nz * two, lanes)).astype(BF16) for x in range(2)]
+            left_a = jnp.concatenate(left_a, 0)
         take_right(rx, 0, g, rr)
         panel_a, panel_b = panel(g)
-        total = tn_dot(panel_a(), b2l[...].reshape(2 * nz * two, lanes))
+        total = tn_dot(panel_a(), left_a)
         if g == 0:
             take(b2lf.at[0], rl.at[1])
-            lefts = [unfold(b2lf[x, k].astype(F32)) for x in range(2) for k in range(nz)]
-            left_b = jnp.concatenate(lefts, 0).astype(BF16)
+            lefts = [jnp.concatenate([unfold(b2lf[x, k].astype(F32)) for k in range(nz)], 0) for x in range(2)]
+            left_b = jnp.concatenate([nn_dot(swap2, left.astype(BF16)).astype(BF16) for left in lefts], 0)
         take_right(rxf, 1, g, rr)
         total = total + tn_dot(panel_b(), left_b)
         pp[low * rows:high * rows] = total[low * rows:high * rows]
@@ -324,7 +326,7 @@
             tri = (pp[pl.ds(k * rows + core * cols, cols), :] + qq[k]) * scale
             for o in range(ny):
                 sc[k, o] = tile(tri, o).astype(BF16)
-            for d in far_first(ny):
+            for d in far_first(ny)[::-1]:
                 to = at_y(d)
                 send(sc.at[k, to], land.at[mine], s3, r3, (to * 2 + xh, k * 4 + xl * 2 + core))
 
@@ -332,6 +334,18 @@
             def _():
                 send(sc.at[k, y], land.at[mine], s3, r3, dev_z(k))
     land[mine] = sc[z, y]
+
+    for part, (first, second, third) in enumerate(((a1l, a2l, rx), (a1lf, a2lf, rxf))):
+        take(first.at[pl.ds(0, ny - 1)], s1l.at[part])
+        take(first.at[pl.ds(0, nz - 1)], s1r.at[part])
+        take(second.at[pl.ds(0, nz - 1)], s2l.at[part])
+        take(second.at[pl.ds(0, ny - 1)], s2r.at[part])
+        take(third.at[0], sl.at[part])
+
+        for g in range(2):
+            take_right(third, part, g, sr)
+    for g, (low, high) in enumerate(groups):
+        take(qq.at[pl.ds(low, high - low)], sq.at[g])
 
     take(land.at[pl.ds(0, chans - 1)], r3)
     f32[...] = land[...].astype(F32).reshape(f32.shape)
@@ -347,17 +361,6 @@
             t, at = j // ny, j % ny * rows
             out[j] = (gate[t, at:at + rows, :] * mixed[start:start + rows]).astype(BF16)
 
-    for part, (first, second, third) in enumerate(((a1l, a2l, rx), (a1lf, a2lf, rxf))):
-        take(first.at[pl.ds(0, ny - 1)], s1l.at[part])
-        take(first.at[pl.ds(0, nz - 1)], s1r.at[part])
-        take(second.at[pl.ds(0, nz - 1)], s2l.at[part])
-        take(second.at[pl.ds(0, ny - 1)], s2r.at[part])
-        take(third.at[0], sl.at[part])
-
-        for g in range(2):
-            take_right(third, part, g, sr)
-    for g, (low, high) in enumerate(groups):
-        take(qq.at[pl.ds(low, high - low)], sq.at[g])
     take(land.at[pl.ds(0, chans - 1)], s3)
 
 
@@ -375,7 +378,7 @@
         out_specs=pl.BlockSpec(memory_space=pltpu.VMEM),
         scratch_shapes=[
             pltpu.SMEM(token_mask.shape, jnp.int32),
-            pltpu.VMEM(pair.shape, BF16),
+            pltpu.VMEM((rows * cols, width), BF16),
             pltpu.VMEM((1, width), F32),
             pltpu.VMEM((1, width), F32),
             pltpu.VMEM(w_left.shape, BF16),
@@ -414,7 +417,7 @@
         compiler_params=pltpu.CompilerParams(
             collective_id=0, has_side_effects=True, vmem_limit_bytes=60 * 1024 * 1024
         ),
-    )(token_mask, pair, ln_gain.reshape(1, width), ln_bias.reshape(1, width), w_left, w_right, w_gate, w_out)
+    )(token_mask, pair.reshape(rows * cols, width), ln_gain.reshape(1, width), ln_bias.reshape(1, width), w_left, w_right, w_gate, w_out)
     return jnp.transpose(swapped, (1, 0, 2))
 
 

time: 40.9 us -> 40.8 us (level)
  no operation moved by 1% of the time
where the time goes in v7:
time: 40.8 us; the launch traced here: 40.7 us
  Pallas kernels  39.9 us (98%)
  local copies, waits for them, and re-layouts  0.79 us (2%)
    pallas_call x1, Pallas kernels, per_device(): pl.pallas_call(functools.partial(kernel, ny, nz), out_shape=pltpu.VMEM((c...  39.9 us

profile of v7, /device:TPU:1, one launch (start us, length us, event | category | flops | bytes accessed | tf_op | source)
XLA Modules:
  0.0 40.7 jit_solution(1402945669297437822)
XLA Ops:
  0.0 39.9 %shard_map.82 = bf16[24,48,128]{2,1,0:T(8,128)(2,1)S(1)} custom-call(s32[768]{0:T(1024)} %tm_hbm.1, bf16[1152,128]{1,0:T(8,128)(2,1)} %bitcast.5, f32[1,128]{1,0:T(1,128)} %bitcast.6, f32[1,128]{1,0:T(1,128)} %bitcast.7, bf16[128,128]{1,0:T(8,128)(2,1)} %wl_hbm.1, bf16[128,128]{1,0:T(8,128)(2,1)} %wr_hbm.1, bf16[128,128]{1,0:T(8,128)(2,1)} %wg_hbm.1, ...), custom_call_target="tpu_custom_call" | custom-call | tf_op jit(solution)/shard_map/pallas_call | solution.py:374
  39.9 0.8 %copy.9 = bf16[48,24,128]{2,1,0:T(8,128)(2,1)} copy(bf16[48,24,128]{2,0,1:T(8,128)(2,1)S(1)} %bitcast.4) | data formatting | bytes 589824 | tf_op jit(solution)/shard_map/transpose | solution.py:421

commit v8 on v7

--- a/solution.py
+++ b/solution.py
@@ -175,7 +175,6 @@
         for d in far_first(ny):
             to = at_y(d)
             send(left.at[to], left_land.at[y], s1l.at[part], r1l.at[part], dev_y(to))
-        for d in far_first(nz):
             to = at_z(d)
             send(right.at[to], right_land.at[z], s1r.at[part], r1r.at[part], dev_z(to))
         left_land[y] = left[y]
@@ -221,17 +220,15 @@
     for k in range(nz):
         a2lf[k] = fold(turned[k * ny:(k + 1) * ny]).astype(BF16)
     send_left(a2lf, b2lf, 1)
+    def forward_left(left, part, k):
+        send(left.at[xl, k], left.at[xl, k], sl.at[part], rl.at[part], dev_x(xh, 1 - xl))
+
+    forward_left(b2l, 0, z)
     turn_right(b1rf, 1, a2rf, b2rf)
-
-    for t in range(nt):
-        gate[t] = jax.nn.sigmoid(nn_dot(normed[t], w_gate[...]))
 
     ahead = max(1, lanes // (3 * rows))
     cut = -(-ahead * rows * 3 // lanes) * (lanes // 3)
     groups = ((0, ahead), (ahead, nz))
-
-    def forward_left(left, part, k):
-        send(left.at[xl, k], left.at[xl, k], sl.at[part], rl.at[part], dev_x(xh, 1 - xl))
 
     def forward_right(right, dst, part, g):
         low, high = groups[g]
@@ -251,7 +248,8 @@
             dst[xl, low:high] = right[low:high]
 
     for part, (left, right, dst) in enumerate(((b2l, b2r, rx), (b2lf, b2rf, rxf))):
-        forward_left(left, part, z)
+        if part:
+            forward_left(left, part, z)
         order = far_first(nz)[::-1]
         for place, d in enumerate(order):
             if place == len(order) // 2:
@@ -334,6 +332,9 @@
             def _():
                 send(sc.at[k, y], land.at[mine], s3, r3, dev_z(k))
     land[mine] = sc[z, y]
+
+    for t in range(nt):
+        gate[t] = jax.nn.sigmoid(nn_dot(normed[t], w_gate[...]))
 
     for part, (first, second, third) in enumerate(((a1l, a2l, rx), (a1lf, a2lf, rxf))):
         take(first.at[pl.ds(0, ny - 1)], s1l.at[part])

time: 40.8 us -> 40.8 us (level)
  no operation moved by 1% of the time
where the time goes in v8:
time: 40.8 us; the launch traced here: 40.7 us
  Pallas kernels  39.9 us (98%)
  local copies, waits for them, and re-layouts  0.79 us (2%)
    pallas_call x1, Pallas kernels, per_device(): pl.pallas_call(functools.partial(kernel, ny, nz), out_shape=pltpu.VMEM((c...  39.9 us

profile of v8, /device:TPU:1, one launch (start us, length us, event | category | flops | bytes accessed | tf_op | source)
XLA Modules:
  0.0 40.7 jit_solution(6952582610821483496)
XLA Ops:
  0.0 39.9 %shard_map.82 = bf16[24,48,128]{2,1,0:T(8,128)(2,1)S(1)} custom-call(s32[768]{0:T(1024)} %tm_hbm.1, bf16[1152,128]{1,0:T(8,128)(2,1)} %bitcast.5, f32[1,128]{1,0:T(1,128)} %bitcast.6, f32[1,128]{1,0:T(1,128)} %bitcast.7, bf16[128,128]{1,0:T(8,128)(2,1)} %wl_hbm.1, bf16[128,128]{1,0:T(8,128)(2,1)} %wr_hbm.1, bf16[128,128]{1,0:T(8,128)(2,1)} %wg_hbm.1, ...), custom_call_target="tpu_custom_call" | custom-call | tf_op jit(solution)/shard_map/pallas_call | solution.py:375
  39.9 0.8 %copy.9 = bf16[48,24,128]{2,1,0:T(8,128)(2,1)} copy(bf16[48,24,128]{2,0,1:T(8,128)(2,1)S(1)} %bitcast.4) | data formatting | bytes 589824 | tf_op jit(solution)/shard_map/transpose | solution.py:422

commit v9 on v8

--- a/solution.py
+++ b/solution.py
@@ -186,13 +186,13 @@
     pairs = lambda u, v, n: jnp.concatenate([u.reshape(n, -1, lanes), v.reshape(n, -1, lanes)], 1).astype(BF16)
     a1l[...] = pairs(left0, left1, ny)
     a1r[...] = pairs(right0, right1, nz)
-    pl.semaphore_wait(barrier, len(peers))
-    send_first(a1l, b1l, a1r, b1r, 0)
     left2, right2 = project(2)
     for k in range(ny):
         a1lf[k] = fold(left2[k * nz:(k + 1) * nz]).astype(BF16)
     for k in range(nz):
         a1rf[k] = fold(right2[k * ny:(k + 1) * ny]).astype(BF16)
+    pl.semaphore_wait(barrier, len(peers))
+    send_first(a1l, b1l, a1r, b1r, 0)
     send_first(a1lf, b1lf, a1rf, b1rf, 1)
 
     def turn_right(land, part, out_buf, dst):

time: 40.8 us -> 40.9 us (level)
  no operation moved by 1% of the time
where the time goes in v9:
time: 40.9 us; the launch traced here: 40.7 us
  Pallas kernels  39.9 us (98%)
  local copies, waits for them, and re-layouts  0.79 us (2%)
    pallas_call x1, Pallas kernels, per_device(): pl.pallas_call(functools.partial(kernel, ny, nz), out_shape=pltpu.VMEM((c...  39.9 us

profile of v9, /device:TPU:1, one launch (start us, length us, event | category | flops | bytes accessed | tf_op | source)
XLA Modules:
  0.0 40.7 jit_solution(16294338458004054223)
XLA Ops:
  0.0 39.9 %shard_map.82 = bf16[24,48,128]{2,1,0:T(8,128)(2,1)S(1)} custom-call(s32[768]{0:T(1024)} %tm_hbm.1, bf16[1152,128]{1,0:T(8,128)(2,1)} %bitcast.5, f32[1,128]{1,0:T(1,128)} %bitcast.6, f32[1,128]{1,0:T(1,128)} %bitcast.7, bf16[128,128]{1,0:T(8,128)(2,1)} %wl_hbm.1, bf16[128,128]{1,0:T(8,128)(2,1)} %wr_hbm.1, bf16[128,128]{1,0:T(8,128)(2,1)} %wg_hbm.1, ...), custom_call_target="tpu_custom_call" | custom-call | tf_op jit(solution)/shard_map/pallas_call | solution.py:375
  40.0 0.8 %copy.9 = bf16[48,24,128]{2,1,0:T(8,128)(2,1)} copy(bf16[48,24,128]{2,0,1:T(8,128)(2,1)S(1)} %bitcast.4) | data formatting | bytes 589824 | tf_op jit(solution)/shard_map/transpose | solution.py:422
